TPU v7x, 128 devices: a whole 4x4x4 slice. The times are simulated.
128 devices in a mesh: tile: 16 (over z, y_hi, core), spec: 8 (over y_lo, x).
Axes of the slice: x: 4, y: 4 (y_hi: 2, y_lo: 2; y = y_hi * 2 + y_lo), z: 4, core: 2. Of those that a mesh axis runs over, the one named last changes fastest.
Arguments:
- tracer: float32 [256, 8, 96, 1440], P('spec', None, 'tile'), may hold values from -6 to 6
- air_mass: float32 [8, 96, 1440], P('spec', 'tile'), may hold values from 2 to 4
- zonal_flux: float32 [8, 96, 1440], P('spec', 'tile'), may hold values from -1.6 to 1.6, as said below
- meridional_flux: float32 [8, 96, 1440], P('spec', 'tile'), may hold values from -0.15 to 0.15
- substeps: int32 [96], replicated, may hold values from 1 to 4, as said below
Outputs:
- tracer_out: float32 [256, 8, 96, 1440], P('spec', None, 'tile')
- mass_out: float32 [8, 96, 1440], P(None, 'tile')
Inputs may be any that keep to these rules, and one draw needn't show every extreme that they name: `substeps`: the count of latitude row j is 1 + (j * 4) // 96 or one more, never over 4; the last row has 4. `zonal_flux`: each entry has magnitude at most 0.4 times its row's substep count, and two neighbouring entries of a row differ by at most 0.2 times that count.
All inputs are finite; a program needn't handle non-finite values.
Results may differ from a plain program's by a relative error of at most 0.0003.
Values sent between devices are 32-bit elements; how exact they have to be, the bound alone decides.
A program may use at most 320 MiB of HBM per device.

v0:
```python
import jax
import jax.numpy as jnp
from jax import lax
from jax.sharding import PartitionSpec as P


def padded(value, sides, width):
    for axis, dim in sides:
        count, length = (lax.axis_size(axis), value.shape[dim])
        up = [(i, (i + 1) % count) for i in range(count - 1)]
        down = [(j, i) for i, j in up]
        last = lax.slice_in_dim(value, length - width, length, axis=dim)
        initial = lax.slice_in_dim(value, 0, width, axis=dim)
        before = lax.ppermute(last, axis, up)
        after = lax.ppermute(initial, axis, down)
        value = jnp.concatenate([before, value, after], axis=dim)
    return value


def limited(back, fore):
    size = jnp.minimum(
        jnp.minimum(2.0 * jnp.abs(back), 2.0 * jnp.abs(fore)), 0.5 * jnp.abs(back + fore)
    )
    return jnp.where(back * fore > 0, jnp.sign(back) * size, 0.0)


def zonal_step(ratio, mass, flux):
    west = jnp.roll(ratio, 1, -1)
    slope = limited(ratio - west, jnp.roll(ratio, -1, -1) - ratio)
    west_mass = jnp.roll(mass, 1, -1)
    upwind = west + 0.5 * (1.0 - flux / west_mass) * jnp.roll(slope, 1, -1)
    downwind = ratio - 0.5 * (1.0 + flux / mass) * slope
    carried = flux * jnp.where(flux > 0, upwind, downwind)
    new_mass = mass + flux - jnp.roll(flux, -1, -1)
    new_ratio = (mass * ratio + carried - jnp.roll(carried, -1, -1)) / new_mass
    return (new_ratio, new_mass)


def zonal_sweep(ratio, mass, flux, counts):
    shares = flux / counts.astype(jnp.float32)[:, None]

    def advance(step, carry):
        cur_ratio, cur_mass = carry
        new_ratio, new_mass = zonal_step(cur_ratio, cur_mass, shares)
        active = (step < counts)[:, None]
        return (jnp.where(active, new_ratio, cur_ratio), jnp.where(active, new_mass, cur_mass))

    return lax.fori_loop(0, jnp.max(counts), advance, (ratio, mass))


def meridional_sweep(ext_ratio, ext_mass, ext_flux, first_row, total_rows):
    rows = ext_ratio.shape[2] - 4
    back = ext_ratio[:, :, 1 : rows + 3] - ext_ratio[:, :, 0 : rows + 2]
    fore = ext_ratio[:, :, 2 : rows + 4] - ext_ratio[:, :, 1 : rows + 3]
    slope = limited(back, fore)
    face_index = first_row + jnp.arange(rows + 1)
    valid = ((face_index > 0) & (face_index < total_rows))[:, None]
    flux = jnp.where(valid, ext_flux[:, 2 : rows + 3], 0.0)
    upwind = (
        ext_ratio[:, :, 1 : rows + 2]
        + 0.5 * (1.0 - flux / ext_mass[:, 1 : rows + 2]) * slope[:, :, 0 : rows + 1]
    )
    downwind = (
        ext_ratio[:, :, 2 : rows + 3]
        - 0.5 * (1.0 + flux / ext_mass[:, 2 : rows + 3]) * slope[:, :, 1 : rows + 2]
    )
    carried = flux * jnp.where(flux > 0, upwind, downwind)
    centre_mass = ext_mass[:, 2 : rows + 2]
    new_mass = centre_mass + flux[:, :rows] - flux[:, 1:]
    new_ratio = (
        centre_mass * ext_ratio[:, :, 2 : rows + 2] + carried[:, :, :rows] - carried[:, :, 1:]
    ) / new_mass
    return (new_ratio, new_mass)


def edge_rows(extended, first_row, total_rows):
    rows = extended.shape[2] - 4
    global_rows = (first_row - 2 + jnp.arange(rows + 4))[:, None]
    lower = jnp.where(global_rows < 0, extended[:, :, 2:3], extended)
    return jnp.where(global_rows >= total_rows, extended[:, :, rows + 1 : rows + 2], lower)


def shards(tracer, air_mass, zonal_flux, meridional_flux, substeps):
    species = tracer.shape[0]
    rows = tracer.shape[2]
    first_row = lax.axis_index("tile") * rows
    total_rows = rows * lax.axis_size("tile")
    mass, eastward, northward = (
        lax.all_gather(air_mass, "spec", axis=0, tiled=True),
        lax.all_gather(zonal_flux, "spec", axis=0, tiled=True),
        lax.all_gather(meridional_flux, "spec", axis=0, tiled=True),
    )
    counts = lax.dynamic_slice_in_dim(substeps, first_row, rows)
    zonal_ratio, zonal_mass = zonal_sweep(tracer, mass, eastward, counts)
    stacked = jnp.concatenate([zonal_ratio, zonal_mass[None], northward[None]], 0)
    extended = padded(stacked, (("tile", 2),), 2)
    extended = edge_rows(extended, first_row, total_rows)
    ext_ratio = extended[:species]
    ext_mass = extended[species]
    ext_flux = extended[species + 1]
    return meridional_sweep(ext_ratio, ext_mass, ext_flux, first_row, total_rows)


def solution(mesh):
    placed = (
        P("spec", None, "tile", None),
        P("spec", "tile", None),
        P("spec", "tile", None),
        P("spec", "tile", None),
        P(),
    )
    return jax.shard_map(
        shards,
        mesh=mesh,
        in_specs=placed,
        out_specs=(P("spec", None, "tile", None), P(None, "tile", None)),
        check_vma=False,
    )
```

profile of v0, /device:TPU:102, one launch (start us, length us, event | category | flops | bytes accessed | tf_op | source)
XLA Modules:
  0.0 487.5 jit_solution(5277832066569224085)
XLA Ops:
  0.7 8.8 %copy.25 = f32[32,8,6,1440]{3,1,2,0:T(8,128)} copy(f32[32,8,6,1440]{3,1,2,0:T(8,128)} %param.7) | data formatting | bytes 17694720
  9.5 28.6 %all_gather.10 = f32[8,6,1440]{2,1,0:T(8,128)S(1)} all-gather(f32[1,6,1440]{2,1,0:T(8,128)S(1)} %copy.8), channel_id=1, replica_groups=mesh['tile'=16,'spec'=8] {'spec'}, dimensions={0}, use_global_device_ids=true | all-gather | bytes 311040 | tf_op jit(solution)/shard_map/all_gather | solution.py:90
  39.4 28.7 %all_gather.11 = f32[8,6,1440]{2,1,0:T(8,128)S(1)} all-gather(f32[1,6,1440]{2,1,0:T(8,128)S(1)} %copy.12), channel_id=1, replica_groups=mesh['tile'=16,'spec'=8] {'spec'}, dimensions={0}, use_global_device_ids=true | all-gather | bytes 311040 | tf_op jit(solution)/shard_map/all_gather | solution.py:91
  69.0 28.8 %all_gather.9 = f32[8,6,1440]{2,1,0:T(8,128)S(1)} all-gather(f32[1,6,1440]{2,1,0:T(8,128)S(1)} %copy.7), channel_id=1, replica_groups=mesh['tile'=16,'spec'=8] {'spec'}, dimensions={0}, use_global_device_ids=true | all-gather | bytes 311040 | tf_op jit(solution)/shard_map/all_gather | solution.py:89
  99.6 257.0 %while.13 = (s32[]{:T(128)}, f32[32,8,6,1440]{3,1,2,0:T(8,128)}, f32[8,6,1440]{2,0,1:T(8,128)S(1)}, s32[]{:T(128)}, s32[6]{0:T(128)S(1)}, /*index=5*/f32[8,6,1440]{2,0,1:T(8,128)}, f32[8,6,1440]{2,0,1:T(8,128)}, s32[]{:T(128)}) while((s32[]{:T(128)}, f32[32,8,6,1440]{3,1,2,0:T(8,128)}, f32[8,6,1440]{2,0,1:T(8,128)S(1)}, s32[]{:T(128)}, ...), condition=%wide.region_2.3_spmd, body=%wide.region_1.2_spmd.sunk | while | flops 71539208 | bytes 242390832 | solution.py:48
  103.4 14.6 %fusion.28 = (f32[32,8,6,1439]{3,1,2,0:T(8,128)}, f32[32,8,6,1439]{3,1,2,0:T(8,128)}) fusion(f32[32,8,6,1440]{3,1,2,0:T(8,128)} %get-tuple-element.182), kind=kLoop, calls=%fused_computation.60.clone.1 | loop fusion | bytes 35364864 | tf_op jit(solution)/shard_map/while/body/jit(_roll_static)/slice | solution.py:28
  118.1 11.4 %multiply_select_fusion.3 = f32[32,8,6,1440]{3,1,2,0:T(8,128)S(1)} fusion(f32[32,8,6,1440]{3,1,2,0:T(8,128)S(1)} %bitcast.17, f32[32,8,6,1]{3,1,2,0:T(8,128)} %get-tuple-element.165, f32[32,8,6,1439]{3,1,2,0:T(8,128)} %get-tuple-element.166, f32[32,8,6,1439]{3,1,2,0:T(8,128)} %get-tuple-element.167, f32[32,8,6,1]{3,1,2,0:T(8,128)} %get-tuple-element.168), kind=kLoop, calls=%fused_computation.9.clone.1 | loop fusion | flops 39813120 | bytes 35389440 | tf_op jit(solution)/shard_map/while/body/jit(_where)/select_n | solution.py:24
  130.8 10.8 %fusion.29 = f32[32,8,6,1440]{3,1,2,0:T(8,128)} fusion(f32[32,8,6,1439]{3,1,2,0:T(8,128)S(1)} %bitcast.18, f32[32,8,6,1]{3,1,2,0:T(8,128)S(1)} %slice.246, f32[32,8,6,1440]{3,1,2,0:T(8,128)S(1)} %bitcast.17, f32[32,8,6,1440]{3,1,2,0:T(8,128)S(1)} %multiply_select_fusion.3, f32[32,8,6,1439]{3,1,2,0:T(8,128)} %get-tuple-element.167, ...), kind=kLoop, calls=%fused_computation.5.clone.1 | loop fusion | flops 17694720 | bytes 45135360 | tf_op jit(solution)/shard_map/while/body/mul | solution.py:33
  141.6 9.9 %slice.249 = f32[32,8,6,1439]{3,1,2,0:T(8,128)} slice(f32[32,8,6,1440]{3,1,2,0:T(8,128)} %fusion.29), slice={[0:32], [0:8], [0:6], [1:1440]} | slice | bytes 17682432 | tf_op jit(solution)/shard_map/while/body/jit(_roll_static)/slice | solution.py:35
  151.5 8.6 %fusion.30 = f32[32,8,6,1440]{3,1,2,0:T(8,128)S(1)} fusion(f32[32,8,6,1440]{3,1,2,0:T(8,128)S(1)} %bitcast.17, f32[32,8,6,1]{3,1,2,0:T(8,128)S(1)} %slice-done.3, f32[32,8,6,1439]{3,1,2,0:T(8,128)} %slice.249, f32[32,8,6,1440]{3,1,2,0:T(8,128)} %fusion.29, f32[8,6,1440]{2,0,1:T(8,128)S(1)} %copy-done.4, f32[8,6,1440]{2,0,1:T(8,128)S(1)} %get-tuple-element.183, ...), kind=kLoop, calls=%fused_computation.8.clone.1 | loop fusion | flops 13271040 | bytes 35942408 | tf_op jit(solution)/shard_map/while/body/jit(_where)/select_n | solution.py:46
  167.4 14.6 %fusion.28 = (f32[32,8,6,1439]{3,1,2,0:T(8,128)}, f32[32,8,6,1439]{3,1,2,0:T(8,128)}) fusion(f32[32,8,6,1440]{3,1,2,0:T(8,128)} %get-tuple-element.182), kind=kLoop, calls=%fused_computation.60.clone.1 | loop fusion | bytes 35364864 | tf_op jit(solution)/shard_map/while/body/jit(_roll_static)/slice | solution.py:28
  182.1 11.4 %multiply_select_fusion.3 = f32[32,8,6,1440]{3,1,2,0:T(8,128)S(1)} fusion(f32[32,8,6,1440]{3,1,2,0:T(8,128)S(1)} %bitcast.17, f32[32,8,6,1]{3,1,2,0:T(8,128)} %get-tuple-element.165, f32[32,8,6,1439]{3,1,2,0:T(8,128)} %get-tuple-element.166, f32[32,8,6,1439]{3,1,2,0:T(8,128)} %get-tuple-element.167, f32[32,8,6,1]{3,1,2,0:T(8,128)} %get-tuple-element.168), kind=kLoop, calls=%fused_computation.9.clone.1 | loop fusion | flops 39813120 | bytes 35389440 | tf_op jit(solution)/shard_map/while/body/jit(_where)/select_n | solution.py:24
  194.9 10.8 %fusion.29 = f32[32,8,6,1440]{3,1,2,0:T(8,128)} fusion(f32[32,8,6,1439]{3,1,2,0:T(8,128)S(1)} %bitcast.18, f32[32,8,6,1]{3,1,2,0:T(8,128)S(1)} %slice.246, f32[32,8,6,1440]{3,1,2,0:T(8,128)S(1)} %bitcast.17, f32[32,8,6,1440]{3,1,2,0:T(8,128)S(1)} %multiply_select_fusion.3, f32[32,8,6,1439]{3,1,2,0:T(8,128)} %get-tuple-element.167, ...), kind=kLoop, calls=%fused_computation.5.clone.1 | loop fusion | flops 17694720 | bytes 45135360 | tf_op jit(solution)/shard_map/while/body/mul | solution.py:33
  205.6 9.9 %slice.249 = f32[32,8,6,1439]{3,1,2,0:T(8,128)} slice(f32[32,8,6,1440]{3,1,2,0:T(8,128)} %fusion.29), slice={[0:32], [0:8], [0:6], [1:1440]} | slice | bytes 17682432 | tf_op jit(solution)/shard_map/while/body/jit(_roll_static)/slice | solution.py:35
  215.6 8.6 %fusion.30 = f32[32,8,6,1440]{3,1,2,0:T(8,128)S(1)} fusion(f32[32,8,6,1440]{3,1,2,0:T(8,128)S(1)} %bitcast.17, f32[32,8,6,1]{3,1,2,0:T(8,128)S(1)} %slice-done.3, f32[32,8,6,1439]{3,1,2,0:T(8,128)} %slice.249, f32[32,8,6,1440]{3,1,2,0:T(8,128)} %fusion.29, f32[8,6,1440]{2,0,1:T(8,128)S(1)} %copy-done.4, f32[8,6,1440]{2,0,1:T(8,128)S(1)} %get-tuple-element.183, ...), kind=kLoop, calls=%fused_computation.8.clone.1 | loop fusion | flops 13271040 | bytes 35942408 | tf_op jit(solution)/shard_map/while/body/jit(_where)/select_n | solution.py:46
  231.5 14.6 %fusion.28 = (f32[32,8,6,1439]{3,1,2,0:T(8,128)}, f32[32,8,6,1439]{3,1,2,0:T(8,128)}) fusion(f32[32,8,6,1440]{3,1,2,0:T(8,128)} %get-tuple-element.182), kind=kLoop, calls=%fused_computation.60.clone.1 | loop fusion | bytes 35364864 | tf_op jit(solution)/shard_map/while/body/jit(_roll_static)/slice | solution.py:28
  246.2 11.4 %multiply_select_fusion.3 = f32[32,8,6,1440]{3,1,2,0:T(8,128)S(1)} fusion(f32[32,8,6,1440]{3,1,2,0:T(8,128)S(1)} %bitcast.17, f32[32,8,6,1]{3,1,2,0:T(8,128)} %get-tuple-element.165, f32[32,8,6,1439]{3,1,2,0:T(8,128)} %get-tuple-element.166, f32[32,8,6,1439]{3,1,2,0:T(8,128)} %get-tuple-element.167, f32[32,8,6,1]{3,1,2,0:T(8,128)} %get-tuple-element.168), kind=kLoop, calls=%fused_computation.9.clone.1 | loop fusion | flops 39813120 | bytes 35389440 | tf_op jit(solution)/shard_map/while/body/jit(_where)/select_n | solution.py:24
  258.9 10.8 %fusion.29 = f32[32,8,6,1440]{3,1,2,0:T(8,128)} fusion(f32[32,8,6,1439]{3,1,2,0:T(8,128)S(1)} %bitcast.18, f32[32,8,6,1]{3,1,2,0:T(8,128)S(1)} %slice.246, f32[32,8,6,1440]{3,1,2,0:T(8,128)S(1)} %bitcast.17, f32[32,8,6,1440]{3,1,2,0:T(8,128)S(1)} %multiply_select_fusion.3, f32[32,8,6,1439]{3,1,2,0:T(8,128)} %get-tuple-element.167, ...), kind=kLoop, calls=%fused_computation.5.clone.1 | loop fusion | flops 17694720 | bytes 45135360 | tf_op jit(solution)/shard_map/while/body/mul | solution.py:33
  269.7 9.9 %slice.249 = f32[32,8,6,1439]{3,1,2,0:T(8,128)} slice(f32[32,8,6,1440]{3,1,2,0:T(8,128)} %fusion.29), slice={[0:32], [0:8], [0:6], [1:1440]} | slice | bytes 17682432 | tf_op jit(solution)/shard_map/while/body/jit(_roll_static)/slice | solution.py:35
  279.6 8.6 %fusion.30 = f32[32,8,6,1440]{3,1,2,0:T(8,128)S(1)} fusion(f32[32,8,6,1440]{3,1,2,0:T(8,128)S(1)} %bitcast.17, f32[32,8,6,1]{3,1,2,0:T(8,128)S(1)} %slice-done.3, f32[32,8,6,1439]{3,1,2,0:T(8,128)} %slice.249, f32[32,8,6,1440]{3,1,2,0:T(8,128)} %fusion.29, f32[8,6,1440]{2,0,1:T(8,128)S(1)} %copy-done.4, f32[8,6,1440]{2,0,1:T(8,128)S(1)} %get-tuple-element.183, ...), kind=kLoop, calls=%fused_computation.8.clone.1 | loop fusion | flops 13271040 | bytes 35942408 | tf_op jit(solution)/shard_map/while/body/jit(_where)/select_n | solution.py:46
  295.5 14.6 %fusion.28 = (f32[32,8,6,1439]{3,1,2,0:T(8,128)}, f32[32,8,6,1439]{3,1,2,0:T(8,128)}) fusion(f32[32,8,6,1440]{3,1,2,0:T(8,128)} %get-tuple-element.182), kind=kLoop, calls=%fused_computation.60.clone.1 | loop fusion | bytes 35364864 | tf_op jit(solution)/shard_map/while/body/jit(_roll_static)/slice | solution.py:28
  310.2 11.4 %multiply_select_fusion.3 = f32[32,8,6,1440]{3,1,2,0:T(8,128)S(1)} fusion(f32[32,8,6,1440]{3,1,2,0:T(8,128)S(1)} %bitcast.17, f32[32,8,6,1]{3,1,2,0:T(8,128)} %get-tuple-element.165, f32[32,8,6,1439]{3,1,2,0:T(8,128)} %get-tuple-element.166, f32[32,8,6,1439]{3,1,2,0:T(8,128)} %get-tuple-element.167, f32[32,8,6,1]{3,1,2,0:T(8,128)} %get-tuple-element.168), kind=kLoop, calls=%fused_computation.9.clone.1 | loop fusion | flops 39813120 | bytes 35389440 | tf_op jit(solution)/shard_map/while/body/jit(_where)/select_n | solution.py:24
  323.0 10.8 %fusion.29 = f32[32,8,6,1440]{3,1,2,0:T(8,128)} fusion(f32[32,8,6,1439]{3,1,2,0:T(8,128)S(1)} %bitcast.18, f32[32,8,6,1]{3,1,2,0:T(8,128)S(1)} %slice.246, f32[32,8,6,1440]{3,1,2,0:T(8,128)S(1)} %bitcast.17, f32[32,8,6,1440]{3,1,2,0:T(8,128)S(1)} %multiply_select_fusion.3, f32[32,8,6,1439]{3,1,2,0:T(8,128)} %get-tuple-element.167, ...), kind=kLoop, calls=%fused_computation.5.clone.1 | loop fusion | flops 17694720 | bytes 45135360 | tf_op jit(solution)/shard_map/while/body/mul | solution.py:33
  333.7 9.9 %slice.249 = f32[32,8,6,1439]{3,1,2,0:T(8,128)} slice(f32[32,8,6,1440]{3,1,2,0:T(8,128)} %fusion.29), slice={[0:32], [0:8], [0:6], [1:1440]} | slice | bytes 17682432 | tf_op jit(solution)/shard_map/while/body/jit(_roll_static)/slice | solution.py:35
  343.7 8.6 %fusion.30 = f32[32,8,6,1440]{3,1,2,0:T(8,128)S(1)} fusion(f32[32,8,6,1440]{3,1,2,0:T(8,128)S(1)} %bitcast.17, f32[32,8,6,1]{3,1,2,0:T(8,128)S(1)} %slice-done.3, f32[32,8,6,1439]{3,1,2,0:T(8,128)} %slice.249, f32[32,8,6,1440]{3,1,2,0:T(8,128)} %fusion.29, f32[8,6,1440]{2,0,1:T(8,128)S(1)} %copy-done.4, f32[8,6,1440]{2,0,1:T(8,128)S(1)} %get-tuple-element.183, ...), kind=kLoop, calls=%fused_computation.8.clone.1 | loop fusion | flops 13271040 | bytes 35942408 | tf_op jit(solution)/shard_map/while/body/jit(_where)/select_n | solution.py:46
  356.6 6.7 %pad_maximum_fusion.3 = (f32[34,8,2,1440]{3,1,2,0:T(8,128)}, f32[34,8,2,1440]{3,1,2,0:T(8,128)}) fusion(f32[1,8,6,1440]{3,1,2,0:T(8,128)} %copy.13, f32[1,8,6,1440]{3,1,2,0:T(8,128)S(1)} %bitcast.20, f32[32,8,6,1440]{3,1,2,0:T(8,128)} %get-tuple-element.66), kind=kLoop, calls=%fused_computation.37 | loop fusion | flops 3133440 | bytes 15667200 | tf_op jit(solution)/shard_map/slice | solution.py:12
  370.0 63.7 %collective-permute-done.1 = f32[34,8,2,1440]{3,1,2,0:T(8,128)} collective-permute-done((f32[34,8,2,1440]{3,1,2,0:T(8,128)}, f32[34,8,2,1440]{3,1,2,0:T(8,128)}, u32[]{:S(2)}, u32[]{:S(2)}) %collective-permute-start.1) | collective-permute-done | bytes 3133472 | tf_op jit(solution)/shard_map/ppermute | solution.py:15
  433.8 7.8 %collective-permute-done = f32[34,8,2,1440]{3,1,2,0:T(8,128)} collective-permute-done((f32[34,8,2,1440]{3,1,2,0:T(8,128)}, f32[34,8,2,1440]{3,1,2,0:T(8,128)}, u32[]{:S(2)}, u32[]{:S(2)}) %collective-permute-start) | collective-permute-done | bytes 3133472 | tf_op jit(solution)/shard_map/ppermute | solution.py:14
  441.6 7.5 %fusion.7 = f32[34,8,10,1440]{3,1,2,0:T(8,128)S(1)} fusion(f32[34,8,2,1440]{3,1,2,0:T(8,128)} %collective-permute-done.1, f32[1,8,6,1440]{3,1,2,0:T(8,128)S(1)} %copy-done.6, f32[1,8,6,1440]{3,1,2,0:T(8,128)S(1)} %bitcast.22, f32[32,8,6,1440]{3,1,2,0:T(8,128)} %get-tuple-element.66, f32[34,8,2,1440]{3,1,2,0:T(8,128)} %collective-permute-done, ...), kind=kLoop, calls=%fused_computation.20 | loop fusion | flops 23500800 | bytes 34467860 | tf_op jit(solution)/shard_map/jit(_where)/select_n | solution.py:80
  449.1 11.2 %multiply_select_fusion.1 = f32[32,8,8,1440]{3,1,2,0:T(8,128)} fusion(f32[34,8,10,1440]{3,1,2,0:T(8,128)S(1)} %fusion.7), kind=kLoop, calls=%fused_computation.23 | loop fusion | flops 47185920 | bytes 47185920 | tf_op jit(solution)/shard_map/jit(_where)/select_n | solution.py:24
  460.7 14.9 %fusion.10 = f32[32,8,7,1440]{3,1,2,0:T(8,128)} fusion(f32[32,8,8,1440]{3,1,2,0:T(8,128)} %multiply_select_fusion.1, f32[34,8,10,1440]{3,1,2,0:T(8,128)S(1)} %fusion.7, f32[8,7,1440]{2,0,1:T(8,128)S(1)} %get-tuple-element.108, f32[8,7,1440]{2,0,1:T(8,128)S(1)} %get-tuple-element.107, f32[8,7,1440]{2,0,1:T(8,128)S(1)} %get-tuple-element.92, ...), kind=kLoop, calls=%fused_computation.28 | loop fusion | flops 15482880 | bytes 52657920 | tf_op jit(solution)/shard_map/mul | solution.py:67
  475.6 11.9 %fusion.12 = f32[32,8,6,1440]{3,1,2,0:T(8,128)} fusion(f32[32,8,7,1440]{3,1,2,0:T(8,128)} %fusion.10, f32[34,8,10,1440]{3,1,2,0:T(8,128)S(1)} %fusion.7, f32[8,6,1440]{2,0,1:T(8,128)S(1)} %get-tuple-element.110, f32[8,6,1440]{2,0,1:T(8,128)S(1)} %get-tuple-element.109), kind=kLoop, calls=%fused_computation.32 | loop fusion | flops 8847360 | bytes 35942400 | tf_op jit(solution)/shard_map/div | solution.py:70
  (146 shorter events, 42.8 us)
Async XLA Ops:
  0.6 68.4 %copy-start.10 = (f32[1,6,1440]{2,0,1:T(1,128)S(1)}, f32[1,6,1440]{2,0,1:T(1,128)}, u32[]{:S(2)}) copy-start(f32[1,6,1440]{2,0,1:T(1,128)} %param.8) | copy-start | bytes 103684
  0.7 38.7 %copy-start.9 = (f32[1,6,1440]{2,0,1:T(1,128)S(1)}, f32[1,6,1440]{2,0,1:T(1,128)}, u32[]{:S(2)}) copy-start(f32[1,6,1440]{2,0,1:T(1,128)} %param.10) | copy-start | bytes 103684
  0.7 37.5 %copy-start.11 = (s32[96]{0:T(128)S(1)}, s32[96]{0:T(128)}, u32[]{:S(2)}) copy-start(s32[96]{0:T(128)} %param.11) | copy-start | bytes 1156
  100.5 17.6 %slice-start = ((s8[9437184]{0:T(1024)(128)(4,1)}), s8[4194304]{0:T(1024)(128)(4,1)S(1)}, s32[]{:S(2)}) async-start(s8[9437184]{0:T(1024)(128)(4,1)} %bitcast.16), calls=%async_computation | async-start | bytes 8388608 | tf_op jit(solution)/shard_map/while
  103.4 14.7 %slice-start.1 = ((s8[9437184]{0:T(1024)(128)(4,1)}), s8[4194304]{0:T(1024)(128)(4,1)S(1)}, s32[]{:S(2)}) async-start(s8[9437184]{0:T(1024)(128)(4,1)} %bitcast.16), calls=%async_computation.1 | async-start | bytes 8388608 | tf_op jit(solution)/shard_map/while
  103.4 14.7 %slice-start.2 = ((s8[9437184]{0:T(1024)(128)(4,1)}), s8[1048576]{0:T(1024)(128)(4,1)S(1)}, s32[]{:S(2)}) async-start(s8[9437184]{0:T(1024)(128)(4,1)} %bitcast.16), calls=%async_computation.2 | async-start | bytes 2097152 | tf_op jit(solution)/shard_map/while
  118.0 11.8 %copy-start.2 = (f32[8,6,1440]{2,0,1:T(8,128)S(1)}, f32[8,6,1440]{2,0,1:T(8,128)}, u32[]{:S(2)}) copy-start(f32[8,6,1440]{2,0,1:T(8,128)} %get-tuple-element.194) | copy-start | bytes 829444 | tf_op jit(solution)/shard_map/while
  118.1 11.8 %copy-start.5 = (f32[8,6,1440]{2,0,1:T(8,128)S(1)}, f32[8,6,1440]{2,0,1:T(8,128)}, u32[]{:S(2)}) copy-start(f32[8,6,1440]{2,0,1:T(8,128)} %get-tuple-element.195) | copy-start | bytes 829444 | tf_op jit(solution)/shard_map/while
  118.1 12.8 %copy-start.1 = (f32[32,8,6,1]{3,1,2,0:T(8,128)S(1)}, f32[32,8,6,1]{3,1,2,0:T(8,128)}, u32[]{:S(2)}) copy-start(f32[32,8,6,1]{3,1,2,0:T(8,128)} %get-tuple-element.168) | copy-start | bytes 18436 | tf_op jit(solution)/shard_map/while
  141.6 9.9 %copy-start.4 = (f32[8,6,1440]{2,0,1:T(8,128)S(1)}, f32[8,6,1440]{2,0,1:T(8,128)}, u32[]{:S(2)}) copy-start(f32[8,6,1440]{2,0,1:T(8,128)} %get-tuple-element.171) | copy-start | bytes 829444 | tf_op jit(solution)/shard_map/while
  164.5 17.6 %slice-start = ((s8[9437184]{0:T(1024)(128)(4,1)}), s8[4194304]{0:T(1024)(128)(4,1)S(1)}, s32[]{:S(2)}) async-start(s8[9437184]{0:T(1024)(128)(4,1)} %bitcast.16), calls=%async_computation | async-start | bytes 8388608 | tf_op jit(solution)/shard_map/while
  167.4 14.7 %slice-start.1 = ((s8[9437184]{0:T(1024)(128)(4,1)}), s8[4194304]{0:T(1024)(128)(4,1)S(1)}, s32[]{:S(2)}) async-start(s8[9437184]{0:T(1024)(128)(4,1)} %bitcast.16), calls=%async_computation.1 | async-start | bytes 8388608 | tf_op jit(solution)/shard_map/while
  167.4 14.7 %slice-start.2 = ((s8[9437184]{0:T(1024)(128)(4,1)}), s8[1048576]{0:T(1024)(128)(4,1)S(1)}, s32[]{:S(2)}) async-start(s8[9437184]{0:T(1024)(128)(4,1)} %bitcast.16), calls=%async_computation.2 | async-start | bytes 2097152 | tf_op jit(solution)/shard_map/while
  182.1 11.8 %copy-start.2 = (f32[8,6,1440]{2,0,1:T(8,128)S(1)}, f32[8,6,1440]{2,0,1:T(8,128)}, u32[]{:S(2)}) copy-start(f32[8,6,1440]{2,0,1:T(8,128)} %get-tuple-element.194) | copy-start | bytes 829444 | tf_op jit(solution)/shard_map/while
  182.1 11.8 %copy-start.5 = (f32[8,6,1440]{2,0,1:T(8,128)S(1)}, f32[8,6,1440]{2,0,1:T(8,128)}, u32[]{:S(2)}) copy-start(f32[8,6,1440]{2,0,1:T(8,128)} %get-tuple-element.195) | copy-start | bytes 829444 | tf_op jit(solution)/shard_map/while
  182.1 12.8 %copy-start.1 = (f32[32,8,6,1]{3,1,2,0:T(8,128)S(1)}, f32[32,8,6,1]{3,1,2,0:T(8,128)}, u32[]{:S(2)}) copy-start(f32[32,8,6,1]{3,1,2,0:T(8,128)} %get-tuple-element.168) | copy-start | bytes 18436 | tf_op jit(solution)/shard_map/while
  228.5 17.6 %slice-start = ((s8[9437184]{0:T(1024)(128)(4,1)}), s8[4194304]{0:T(1024)(128)(4,1)S(1)}, s32[]{:S(2)}) async-start(s8[9437184]{0:T(1024)(128)(4,1)} %bitcast.16), calls=%async_computation | async-start | bytes 8388608 | tf_op jit(solution)/shard_map/while
  231.5 14.7 %slice-start.1 = ((s8[9437184]{0:T(1024)(128)(4,1)}), s8[4194304]{0:T(1024)(128)(4,1)S(1)}, s32[]{:S(2)}) async-start(s8[9437184]{0:T(1024)(128)(4,1)} %bitcast.16), calls=%async_computation.1 | async-start | bytes 8388608 | tf_op jit(solution)/shard_map/while
  231.5 14.7 %slice-start.2 = ((s8[9437184]{0:T(1024)(128)(4,1)}), s8[1048576]{0:T(1024)(128)(4,1)S(1)}, s32[]{:S(2)}) async-start(s8[9437184]{0:T(1024)(128)(4,1)} %bitcast.16), calls=%async_computation.2 | async-start | bytes 2097152 | tf_op jit(solution)/shard_map/while
  246.1 11.8 %copy-start.2 = (f32[8,6,1440]{2,0,1:T(8,128)S(1)}, f32[8,6,1440]{2,0,1:T(8,128)}, u32[]{:S(2)}) copy-start(f32[8,6,1440]{2,0,1:T(8,128)} %get-tuple-element.194) | copy-start | bytes 829444 | tf_op jit(solution)/shard_map/while
  246.1 11.8 %copy-start.5 = (f32[8,6,1440]{2,0,1:T(8,128)S(1)}, f32[8,6,1440]{2,0,1:T(8,128)}, u32[]{:S(2)}) copy-start(f32[8,6,1440]{2,0,1:T(8,128)} %get-tuple-element.195) | copy-start | bytes 829444 | tf_op jit(solution)/shard_map/while
  246.2 12.8 %copy-start.1 = (f32[32,8,6,1]{3,1,2,0:T(8,128)S(1)}, f32[32,8,6,1]{3,1,2,0:T(8,128)}, u32[]{:S(2)}) copy-start(f32[32,8,6,1]{3,1,2,0:T(8,128)} %get-tuple-element.168) | copy-start | bytes 18436 | tf_op jit(solution)/shard_map/while
  292.6 17.6 %slice-start = ((s8[9437184]{0:T(1024)(128)(4,1)}), s8[4194304]{0:T(1024)(128)(4,1)S(1)}, s32[]{:S(2)}) async-start(s8[9437184]{0:T(1024)(128)(4,1)} %bitcast.16), calls=%async_computation | async-start | bytes 8388608 | tf_op jit(solution)/shard_map/while
  295.5 14.7 %slice-start.1 = ((s8[9437184]{0:T(1024)(128)(4,1)}), s8[4194304]{0:T(1024)(128)(4,1)S(1)}, s32[]{:S(2)}) async-start(s8[9437184]{0:T(1024)(128)(4,1)} %bitcast.16), calls=%async_computation.1 | async-start | bytes 8388608 | tf_op jit(solution)/shard_map/while
  295.5 14.7 %slice-start.2 = ((s8[9437184]{0:T(1024)(128)(4,1)}), s8[1048576]{0:T(1024)(128)(4,1)S(1)}, s32[]{:S(2)}) async-start(s8[9437184]{0:T(1024)(128)(4,1)} %bitcast.16), calls=%async_computation.2 | async-start | bytes 2097152 | tf_op jit(solution)/shard_map/while
  310.2 11.8 %copy-start.2 = (f32[8,6,1440]{2,0,1:T(8,128)S(1)}, f32[8,6,1440]{2,0,1:T(8,128)}, u32[]{:S(2)}) copy-start(f32[8,6,1440]{2,0,1:T(8,128)} %get-tuple-element.194) | copy-start | bytes 829444 | tf_op jit(solution)/shard_map/while
  310.2 11.8 %copy-start.5 = (f32[8,6,1440]{2,0,1:T(8,128)S(1)}, f32[8,6,1440]{2,0,1:T(8,128)}, u32[]{:S(2)}) copy-start(f32[8,6,1440]{2,0,1:T(8,128)} %get-tuple-element.195) | copy-start | bytes 829444 | tf_op jit(solution)/shard_map/while
  310.2 12.8 %copy-start.1 = (f32[32,8,6,1]{3,1,2,0:T(8,128)S(1)}, f32[32,8,6,1]{3,1,2,0:T(8,128)}, u32[]{:S(2)}) copy-start(f32[32,8,6,1]{3,1,2,0:T(8,128)} %get-tuple-element.168) | copy-start | bytes 18436 | tf_op jit(solution)/shard_map/while
  356.6 11.3 %copy-start.6 = (f32[1,8,6,1440]{3,1,2,0:T(8,128)S(1)}, f32[1,8,6,1440]{3,1,2,0:T(8,128)}, u32[]{:S(2)}) copy-start(f32[1,8,6,1440]{3,1,2,0:T(8,128)} %copy.13) | copy-start | bytes 829444
  363.3 70.5 %collective-permute-start.1 = (f32[34,8,2,1440]{3,1,2,0:T(8,128)}, f32[34,8,2,1440]{3,1,2,0:T(8,128)}, u32[]{:S(2)}, u32[]{:S(2)}) collective-permute-start(f32[34,8,2,1440]{3,1,2,0:T(8,128)} %get-tuple-element.106), channel_id=1, source_target_pairs={{8,0},{16,8},{24,16},{32,24},{40,32},{48,40},{56,48},{64,56},{72,6... | collective-permute-start | bytes 9400328 | tf_op jit(solution)/shard_map/ppermute | solution.py:15
  365.2 76.3 %collective-permute-start = (f32[34,8,2,1440]{3,1,2,0:T(8,128)}, f32[34,8,2,1440]{3,1,2,0:T(8,128)}, u32[]{:S(2)}, u32[]{:S(2)}) collective-permute-start(f32[34,8,2,1440]{3,1,2,0:T(8,128)} %get-tuple-element.105), channel_id=1, source_target_pairs={{0,8},{8,16},{16,24},{24,32},{32,40},{40,48},{48,56},{56,64},{64,7... | collective-permute-start | bytes 9400328 | tf_op jit(solution)/shard_map/ppermute | solution.py:14
  460.7 14.9 %copy-start.7 = (f32[8,6,1440]{2,0,1:T(8,128)}, f32[8,6,1440]{2,0,1:T(8,128)S(1)}, u32[]{:S(2)}) copy-start(f32[8,6,1440]{2,0,1:T(8,128)S(1)} %get-tuple-element.110) | copy-start | bytes 829444
  (16 other events, 127.7 us)
where the time goes:
time: 488 us
  other arithmetic  182 us (37%)
  local copies, waits for them, and re-layouts  138 us (28%)
  blocking collectives  86.2 us (18%)
  waiting for transfers between devices  71.6 us (15%)
    slice x8, local copies, waits for them, and re-layouts, zonal_step(): west = jnp.roll(ratio, 1, -1)  70.2 us
    ppermute x1, waiting for transfers between devices, padded(): after = lax.ppermute(initial, axis, down)  63.7 us
    select_n x5, other arithmetic, limited(): return jnp.where(back * fore > 0, jnp.sign(back) * size, 0.0)  56.9 us
    mul x4, other arithmetic, zonal_step(): carried = flux * jnp.where(flux > 0, upwind, downwind)  43 us
    slice x12, local copies, waits for them, and re-layouts, zonal_step(): new_ratio = (mass * ratio + carried - jnp.roll(carried, -1, -1)) / new_mass  39.7 us
    select_n x4, other arithmetic, advance(): jnp.where(active, new_ratio, cur_ratio)  34.3 us
    all_gather x1, blocking collectives, shards(): lax.all_gather(air_mass, 'spec', axis=0, tiled=True)  28.8 us
    all_gather x1, blocking collectives, shards(): lax.all_gather(meridional_flux, 'spec', axis=0, tiled=True)  28.7 us
  transfers between devices with their start and end apart: 2, of which 2 were waited for; matrix products, arithmetic and copies ran while one was open for 0% of the time, Pallas kernels for 0%

commit v1 on v0

v1 whole, which is shorter than its diff:
```python
import jax
import jax.numpy as jnp
from jax import lax
from jax.experimental import pallas as pl
from jax.experimental.pallas import tpu as pltpu
from jax.sharding import PartitionSpec as P

MESH = pl.DeviceIdType.MESH
NX = 1440
WIDE = 1536
LANES = 128
LEVELS = 8
ROWS = 6
STEPS = 4
GROUP = 2


def widened(row):
    return jnp.concatenate([row, row[:, :48], row[:, NX - 48 :]], axis=1)


def east(value):
    return pltpu.roll(value, WIDE - 1, 1)


def west(value):
    return pltpu.roll(value, 1, 1)


def half_slope(back, fore):
    low = jnp.maximum(jnp.minimum(back, fore), 0.0)
    high = jnp.minimum(jnp.maximum(back, fore), 0.0)
    return jnp.maximum(jnp.minimum(0.25 * (back + fore), low), high)


def kernel(
    tiles,
    tracer,
    air,
    zonal,
    merid,
    substeps,
    out,
    mass_out,
    landed,
    swept,
    gathered,
    whole,
    coef,
    last_mass,
    from_south,
    from_north,
    edge_south,
    edge_north,
    got_south,
    got_north,
    faces,
    cells,
    load_sem,
    gather_send,
    gather_recv,
    send_north,
    send_south,
    recv_south,
    recv_north,
    edge_send,
    edge_recv,
):
    tile = lax.axis_index("tile")
    spec = lax.axis_index("spec")
    groups = tracer.shape[0] // GROUP
    has_south = tile > 0
    has_north = tile < tiles - 1

    def load(group):
        part = pl.ds(group * GROUP, GROUP)
        return pltpu.make_async_copy(tracer.at[part], landed.at[part], load_sem.at[group])

    def start_load(group, carry):
        load(group).start()
        return carry

    lax.fori_loop(0, groups, start_load, 0)

    barrier = pltpu.get_barrier_semaphore()
    for step in range(1, LEVELS):
        peer = lax.rem(spec + step, LEVELS)
        pl.semaphore_signal(barrier, inc=1, device_id=(tile, peer), device_id_type=MESH)

    @pl.when(has_south)
    def _():
        pl.semaphore_signal(barrier, inc=1, device_id=(tile - 1, spec), device_id_type=MESH)

    @pl.when(has_north)
    def _():
        pl.semaphore_signal(barrier, inc=1, device_id=(tile + 1, spec), device_id_type=MESH)

    greeted = LEVELS - 1 + has_south.astype(jnp.int32) + has_north.astype(jnp.int32)
    pl.semaphore_wait(barrier, greeted)

    sources = (air, zonal, merid)

    def give(index, step):
        peer = lax.rem(spec + step, LEVELS)
        return pltpu.make_async_remote_copy(
            src_ref=sources[index],
            dst_ref=gathered.at[index, spec],
            send_sem=gather_send.at[index, step],
            recv_sem=gather_recv.at[index, spec],
            device_id=(tile, peer),
            device_id_type=MESH,
        )

    for step in range(1, LEVELS):
        for index in range(3):
            give(index, step).start()
    for index in range(3):
        gathered[index, spec] = sources[index][...]
    for step in range(1, LEVELS):
        level = lax.rem(spec + LEVELS - step, LEVELS)
        for index in range(3):
            pltpu.make_async_remote_copy(
                src_ref=sources[index],
                dst_ref=gathered.at[index, level],
                send_sem=gather_send.at[index, step],
                recv_sem=gather_recv.at[index, level],
                device_id=(tile, level),
                device_id_type=MESH,
            ).wait()
    for index in range(3):
        for level in range(LEVELS):
            for row in range(ROWS):
                whole[index, row, level : level + 1, :] = gathered[index, level, row]

    first = tile * ROWS

    def prepare(row, carry):
        count = substeps[first + row]
        share = widened(whole[1, row]) / count.astype(jnp.float32)
        mass = widened(whole[0, row])
        for step in range(STEPS):
            flux = jnp.where(step < count, share, 0.0)
            inner = jnp.where(
                flux > 0, 1.0 - flux / west(mass), -1.0 - flux / mass
            )
            coef[row, step, 0] = flux
            coef[row, step, 1] = inner
            coef[row, step, 2] = mass
            mass = mass + flux - east(flux)
            coef[row, step, 3] = 1.0 / mass
        last_mass[row] = mass
        return carry

    lax.fori_loop(0, ROWS, prepare, 0)

    edge_north[0] = last_mass[ROWS - 1]
    edge_south[0] = last_mass[0]
    edge_south[1] = widened(whole[2, 0])

    def edge_up():
        return pltpu.make_async_remote_copy(
            src_ref=edge_north,
            dst_ref=got_south,
            send_sem=edge_send.at[0],
            recv_sem=edge_recv.at[0],
            device_id=(tile + 1, spec),
            device_id_type=MESH,
        )

    def edge_down():
        return pltpu.make_async_remote_copy(
            src_ref=edge_south,
            dst_ref=got_north,
            send_sem=edge_send.at[1],
            recv_sem=edge_recv.at[1],
            device_id=(tile - 1, spec),
            device_id_type=MESH,
        )

    pl.when(has_north)(lambda: edge_up().start())
    pl.when(has_south)(lambda: edge_down().start())

    def up(group):
        return pltpu.make_async_remote_copy(
            src_ref=swept.at[pl.ds(group * GROUP, GROUP), pl.ds(ROWS - 2, 2)],
            dst_ref=from_south.at[group],
            send_sem=send_north.at[group],
            recv_sem=recv_south.at[group],
            device_id=(tile + 1, spec),
            device_id_type=MESH,
        )

    def down(group):
        return pltpu.make_async_remote_copy(
            src_ref=swept.at[pl.ds(group * GROUP, GROUP), pl.ds(0, 2)],
            dst_ref=from_north.at[group],
            send_sem=send_south.at[group],
            recv_sem=recv_north.at[group],
            device_id=(tile - 1, spec),
            device_id_type=MESH,
        )

    def sweep_row(species, row):
        ratio = widened(landed[species, row])
        for step in range(STEPS):
            flux = coef[row, step, 0]
            fore = east(ratio) - ratio
            back = west(fore)
            slope = half_slope(back, fore)
            eastward = flux > 0
            value = jnp.where(eastward, ratio - back, ratio) + coef[row, step, 1] * jnp.where(
                eastward, west(slope), slope
            )
            carried = flux * value
            ratio = (coef[row, step, 2] * ratio + carried - east(carried)) * coef[row, step, 3]
        swept[species, row] = ratio

    def zonal_group(group, carry):
        load(group).wait()

        def one_row(row, inner):
            for species in range(GROUP):
                sweep_row(group * GROUP + species, row)
            return inner

        lax.fori_loop(0, ROWS, one_row, 0)
        pl.when(has_north)(lambda: up(group).start())
        pl.when(has_south)(lambda: down(group).start())
        return carry

    lax.fori_loop(0, groups, zonal_group, 0)

    @pl.when(has_south)
    def _():
        edge_down().wait_send()
        edge_up().wait_recv()

    @pl.when(has_north)
    def _():
        edge_up().wait_send()
        edge_down().wait_recv()

    @pl.when(jnp.logical_not(has_south))
    def _():
        got_south[0] = last_mass[0]

    @pl.when(jnp.logical_not(has_north))
    def _():
        got_north[0] = last_mass[ROWS - 1]
        got_north[1] = jnp.zeros((LEVELS, WIDE), jnp.float32)

    masses = [got_south[0]] + [last_mass[row] for row in range(ROWS)] + [got_north[0]]
    fluxes = [jnp.where(has_south, widened(whole[2, 0]), 0.0)]
    fluxes += [widened(whole[2, row]) for row in range(1, ROWS)] + [got_north[1]]
    for face in range(ROWS + 1):
        flux = fluxes[face]
        faces[face, 0] = flux
        faces[face, 1] = jnp.where(
            flux > 0, 1.0 - flux / masses[face], -1.0 - flux / masses[face + 1]
        )
    for row in range(ROWS):
        mass = masses[row + 1] + fluxes[row] - fluxes[row + 1]
        cells[row, 0] = masses[row + 1]
        cells[row, 1] = 1.0 / mass
        mass_out[row] = mass[:, :NX]

    def merid_part(group, species, start, width):
        lanes = pl.ds(start, width)
        own = group * GROUP + species
        rows = [from_south[group, species, k, :, lanes] for k in range(2)]
        rows += [swept[own, row, :, lanes] for row in range(ROWS)]
        rows += [from_north[group, species, k, :, lanes] for k in range(2)]
        diffs = [rows[k + 1] - rows[k] for k in range(ROWS + 3)]
        slopes = [half_slope(diffs[k], diffs[k + 1]) for k in range(ROWS + 2)]
        carried = []
        for face in range(ROWS + 1):
            flux = faces[face, 0, :, lanes]
            northward = flux > 0
            value = jnp.where(northward, rows[face + 1], rows[face + 2]) + faces[
                face, 1, :, lanes
            ] * jnp.where(northward, slopes[face], slopes[face + 1])
            carried.append(flux * value)
        for row in range(ROWS):
            out[own, row, :, lanes] = (
                cells[row, 0, :, lanes] * rows[row + 2] + carried[row] - carried[row + 1]
            ) * cells[row, 1, :, lanes]

    full = NX // LANES

    def merid_group(group, carry):
        @pl.when(has_south)
        def _():
            up(group).wait_recv()
            down(group).wait_send()

        @pl.when(has_north)
        def _():
            down(group).wait_recv()
            up(group).wait_send()

        for species in range(GROUP):

            @pl.when(jnp.logical_not(has_south))
            def _():
                for k in range(2):
                    from_south[group, species, k] = swept[group * GROUP + species, 0]

            @pl.when(jnp.logical_not(has_north))
            def _():
                for k in range(2):
                    from_north[group, species, k] = swept[group * GROUP + species, ROWS - 1]

        def block(index, inner):
            for species in range(GROUP):
                merid_part(group, species, pl.multiple_of(index * LANES, LANES), LANES)
            return inner

        lax.fori_loop(0, full, block, 0)
        for species in range(GROUP):
            merid_part(group, species, full * LANES, NX - full * LANES)
        return carry

    lax.fori_loop(0, groups, merid_group, 0)


def shards(tiles, tracer, air_mass, zonal_flux, meridional_flux, substeps):
    species = tracer.shape[0]
    groups = species // GROUP
    rows_first = [jnp.transpose(x, (1, 0, 2)) for x in (air_mass, zonal_flux, meridional_flux)]
    f32 = jnp.float32
    dma = pltpu.SemaphoreType.DMA

    def body(*refs):
        kernel(tiles, *refs)

    vmem = pl.BlockSpec(memory_space=pltpu.VMEM)
    ratios, masses = pl.pallas_call(
        body,
        out_shape=(
            jax.ShapeDtypeStruct((species, ROWS, LEVELS, NX), f32),
            jax.ShapeDtypeStruct((ROWS, LEVELS, NX), f32),
        ),
        in_specs=[pl.BlockSpec(memory_space=pl.ANY), vmem, vmem, vmem, pl.BlockSpec(memory_space=pltpu.SMEM)],
        out_specs=(vmem, vmem),
        scratch_shapes=[
            pltpu.VMEM((species, ROWS, LEVELS, NX), f32),
            pltpu.VMEM((species, ROWS, LEVELS, WIDE), f32),
            pltpu.VMEM((3, LEVELS, ROWS, 1, NX), f32),
            pltpu.VMEM((3, ROWS, LEVELS, NX), f32),
            pltpu.VMEM((ROWS, STEPS, 4, LEVELS, WIDE), f32),
            pltpu.VMEM((ROWS, LEVELS, WIDE), f32),
            pltpu.VMEM((groups, GROUP, 2, LEVELS, WIDE), f32),
            pltpu.VMEM((groups, GROUP, 2, LEVELS, WIDE), f32),
            pltpu.VMEM((2, LEVELS, WIDE), f32),
            pltpu.VMEM((1, LEVELS, WIDE), f32),
            pltpu.VMEM((1, LEVELS, WIDE), f32),
            pltpu.VMEM((2, LEVELS, WIDE), f32),
            pltpu.VMEM((ROWS + 1, 2, LEVELS, WIDE), f32),
            pltpu.VMEM((ROWS, 2, LEVELS, WIDE), f32),
            dma((groups,)),
            dma((3, LEVELS)),
            dma((3, LEVELS)),
            dma((groups,)),
            dma((groups,)),
            dma((groups,)),
            dma((groups,)),
            dma((2,)),
            dma((2,)),
        ],
        compiler_params=pltpu.CompilerParams(
            collective_id=0, has_side_effects=True, vmem_limit_bytes=58 * 2**20
        ),
        cost_estimate=pl.CostEstimate(flops=10**9, bytes_accessed=2 * 10**7, transcendentals=0),
    )(jnp.transpose(tracer, (0, 2, 1, 3)), *rows_first, substeps)
    return jnp.transpose(ratios, (0, 2, 1, 3)), jnp.transpose(masses, (1, 0, 2))


def solution(mesh):
    tiles = mesh.shape["tile"]

    def run(*args):
        return shards(tiles, *args)

    placed = (
        P("spec", None, "tile", None),
        P("spec", "tile", None),
        P("spec", "tile", None),
        P("spec", "tile", None),
        P(),
    )
    return jax.shard_map(
        run,
        mesh=mesh,
        in_specs=placed,
        out_specs=(P("spec", None, "tile", None), P(None, "tile", None)),
        check_vma=False,
    )
```

time: 488 us -> 167 us (0.34)
  the two profiles are of different devices: /device:TPU:102 before, /device:TPU:1 now
where the time goes in v1:
time: 167 us
  Pallas kernels  157 us (94%)
  local copies, waits for them, and re-layouts  9.56 us (6%)
    pallas_call x1, Pallas kernels, shards(): pl.pallas_call(body, out_shape=(jax.ShapeDtypeStruct((species, ROWS, LEVE...  157 us
    unnamed x4, local copies, waits for them, and re-layouts  9.56 us

profile of v1, /device:TPU:1, one launch (start us, length us, event | category | flops | bytes accessed | tf_op | source)
XLA Modules:
  0.0 167.1 jit_solution(7341203728876490577)
XLA Ops:
  0.6 156.9 %shard_map.68 = (f32[32,6,8,1440]{3,2,1,0:T(8,128)}, f32[6,8,1440]{2,1,0:T(8,128)}) custom-call(f32[32,6,8,1440]{3,2,1,0:T(8,128)} %bitcast.6, f32[6,1,1440]{2,1,0:T(1,128)} %bitcast.9, f32[6,1,1440]{2,1,0:T(1,128)} %bitcast.10, f32[6,1,1440]{2,1,0:T(1,128)} %bitcast.11, s32[96]{0:T(128)} %refs_4_.1), custom_call_target="tpu_custom_call" | custom-call | flops 1000000000 | bytes 20000000 | tf_op jit(solution)/shard_map/pallas_call | solution.py:337
  157.6 0.0 copy-start
  157.6 8.8 %copy.9 = f32[32,8,6,1440]{3,1,2,0:T(8,128)} copy(f32[32,8,6,1440]{3,1,2,0:T(8,128)} %bitcast.7) | data formatting | bytes 17694720
  166.4 0.0 copy-done
  166.4 0.7 copy.10
Async XLA Ops:
  157.6 8.9 %copy-start = (f32[6,8,1440]{2,1,0:T(8,128)S(1)}, f32[6,8,1440]{2,1,0:T(8,128)}, u32[]{:S(2)}) copy-start(f32[6,8,1440]{2,1,0:T(8,128)} %get-tuple-element.5) | copy-start | bytes 829444

commit v2 on v1

v2 whole, which is shorter than its diff:
```python
import jax
import jax.numpy as jnp
from jax import lax
from jax.experimental import pallas as pl
from jax.experimental.pallas import tpu as pltpu
from jax.sharding import PartitionSpec as P

MESH = pl.DeviceIdType.MESH
NX = 1440
LANES = 128
COLS = 12
WIDE = COLS * LANES
LEVELS = 8
ROWS = 6
STEPS = 4
GROUP = 2
PACK = LANES // LEVELS
FIELD_ROWS = 24
FULL = NX // LANES


def east(value):
    return jnp.concatenate([value[1:], pltpu.roll(value[0], LANES - 1, 1)[None]], axis=0)


def west(value):
    return jnp.concatenate([pltpu.roll(value[COLS - 1], 1, 1)[None], value[: COLS - 1]], axis=0)


def half_slope(back, fore):
    low = jnp.maximum(jnp.minimum(back, fore), 0.0)
    high = jnp.minimum(jnp.maximum(back, fore), 0.0)
    return jnp.maximum(jnp.minimum(0.25 * (back + fore), low), high)


def wrap(turned):
    turned[NX : NX + COLS, :] = turned[0:COLS, :]
    turned[WIDE - COLS : WIDE, :] = turned[NX - COLS : NX, :]


def every(turned, col):
    return turned[pl.ds(col, LANES, stride=COLS), :]


def kernel(
    tiles,
    tracer,
    air,
    zonal,
    merid,
    substeps,
    out,
    mass_out,
    swept,
    turned,
    turned_more,
    back_turned,
    mine,
    gathered,
    levels,
    field,
    coef,
    last_mass,
    from_south,
    from_north,
    edge_south,
    edge_north,
    got_south,
    got_north,
    faces,
    cells,
    masses_new,
    load_sem,
    gather_send,
    gather_recv,
    send_north,
    send_south,
    recv_south,
    recv_north,
    edge_send,
    edge_recv,
):
    tile = lax.axis_index("tile")
    spec = lax.axis_index("spec")
    species = tracer.shape[0]
    groups = species // GROUP
    packs = species // PACK
    has_south = tile > 0
    has_north = tile < tiles - 1

    def load(pack, row):
        part = pl.ds(pack * PACK, PACK)
        return pltpu.make_async_copy(
            tracer.at[part, row], out.at[part, row], load_sem.at[pack * ROWS + row]
        )

    def start_load(index, carry):
        load(index // ROWS, index % ROWS).start()
        return carry

    lax.fori_loop(0, packs * ROWS, start_load, 0)

    half = LEVELS // 2
    partner = lax.rem(spec + half, LEVELS)
    side = (spec // half) * half
    peers = [side + lax.rem(spec + step, half) for step in range(1, half)]

    barrier = pltpu.get_barrier_semaphore()
    for peer in [partner] + peers:
        pl.semaphore_signal(barrier, inc=1, device_id=(tile, peer), device_id_type=MESH)

    @pl.when(has_south)
    def _():
        pl.semaphore_signal(barrier, inc=1, device_id=(tile - 1, spec), device_id_type=MESH)

    @pl.when(has_north)
    def _():
        pl.semaphore_signal(barrier, inc=1, device_id=(tile + 1, spec), device_id_type=MESH)

    mine[...] = jnp.zeros_like(mine)
    for index, source in enumerate((air, zonal, merid)):
        mine[index * ROWS : (index + 1) * ROWS, :] = source[:, 0, :]
    gathered[spec] = mine[...]
    for buffer in (turned, turned_more):
        buffer[NX:WIDE, :] = jnp.ones((WIDE - NX, LANES), jnp.float32)

    greeted = half + has_south.astype(jnp.int32) + has_north.astype(jnp.int32)
    pl.semaphore_wait(barrier, greeted)

    def give(source, level, peer, slot):
        return pltpu.make_async_remote_copy(
            src_ref=source,
            dst_ref=gathered.at[level],
            send_sem=gather_send.at[slot],
            recv_sem=gather_recv.at[level],
            device_id=(tile, peer),
            device_id_type=MESH,
        )

    to_partner = give(mine, spec, partner, 0)
    to_partner.start()
    own = [give(mine, spec, peer, 1 + k) for k, peer in enumerate(peers)]
    for copy in own:
        copy.start()

    def turn_in(pack, row):
        load(pack, row).wait()
        part = pl.ds(pack * PACK, PACK)
        for col in range(FULL):
            lanes = slice(col * LANES, (col + 1) * LANES)
            turned[lanes, :] = out[part, row, :, lanes].reshape(LANES, LANES).T
        rest = slice(FULL * LANES, NX)
        turned[rest, :] = out[part, row, :, rest].reshape(LANES, NX - FULL * LANES).T
        wrap(turned)
        for col in range(COLS):
            swept[part, row, col] = every(turned, col).T.reshape(PACK, LEVELS, LANES)

    def turn_pack(pack):
        def one(row, carry):
            turn_in(pack, row)
            return carry

        lax.fori_loop(0, ROWS, one, 0)

    turn_pack(0)
    pltpu.make_async_remote_copy(
        src_ref=mine,
        dst_ref=gathered.at[partner],
        send_sem=gather_send.at[0],
        recv_sem=gather_recv.at[partner],
        device_id=(tile, partner),
        device_id_type=MESH,
    ).wait()
    passed = [give(gathered.at[partner], partner, peer, half + k) for k, peer in enumerate(peers)]
    for copy in passed:
        copy.start()
    for pack in range(1, packs):
        turn_pack(pack)
    for copy in own + passed:
        copy.wait_send()
    for step in range(1, half):
        level = side + lax.rem(spec + half - step, half)
        for got in (level, lax.rem(level + half, LEVELS)):
            give(mine, got, peers[0], 0).wait_recv()

    more = LEVELS * FIELD_ROWS - LANES
    for col in range(COLS):
        lanes = slice(col * LANES, min((col + 1) * LANES, NX))
        width = lanes.stop - lanes.start
        block = gathered[:, :, lanes].reshape(LEVELS * FIELD_ROWS, width)
        turned[lanes, :] = block[:LANES].T
        turned_more[lanes, 0:more] = block[LANES:].T
    wrap(turned)
    wrap(turned_more)
    for col in range(COLS):
        levels[col, 0:LANES] = every(turned, col).T
        levels[col, LANES : LANES + more] = every(turned_more, col).T[:more]
        for index in range(3):
            for row in range(ROWS):
                field[index, row, col] = levels[
                    col, pl.ds(index * ROWS + row, LEVELS, stride=FIELD_ROWS), :
                ]

    first = tile * ROWS

    def prepare(row, carry):
        count = substeps[first + row]
        share = field[1, row] / count.astype(jnp.float32)
        mass = field[0, row]
        for step in range(STEPS):
            flux = jnp.where(step < count, share, 0.0)
            coef[row, step, 0] = flux
            coef[row, step, 1] = jnp.where(flux > 0, 1.0 - flux / west(mass), -1.0 - flux / mass)
            coef[row, step, 2] = mass
            mass = mass + flux - east(flux)
            coef[row, step, 3] = 1.0 / mass
        last_mass[row] = mass
        return carry

    lax.fori_loop(0, ROWS, prepare, 0)

    edge_north[0] = last_mass[ROWS - 1]
    edge_south[0] = last_mass[0]
    edge_south[1] = field[2, 0]

    def edge_up():
        return pltpu.make_async_remote_copy(
            src_ref=edge_north,
            dst_ref=got_south,
            send_sem=edge_send.at[0],
            recv_sem=edge_recv.at[0],
            device_id=(tile + 1, spec),
            device_id_type=MESH,
        )

    def edge_down():
        return pltpu.make_async_remote_copy(
            src_ref=edge_south,
            dst_ref=got_north,
            send_sem=edge_send.at[1],
            recv_sem=edge_recv.at[1],
            device_id=(tile - 1, spec),
            device_id_type=MESH,
        )

    pl.when(has_north)(lambda: edge_up().start())
    pl.when(has_south)(lambda: edge_down().start())

    def up(group):
        return pltpu.make_async_remote_copy(
            src_ref=swept.at[pl.ds(group * GROUP, GROUP), pl.ds(ROWS - 2, 2)],
            dst_ref=from_south.at[group],
            send_sem=send_north.at[group],
            recv_sem=recv_south.at[group],
            device_id=(tile + 1, spec),
            device_id_type=MESH,
        )

    def down(group):
        return pltpu.make_async_remote_copy(
            src_ref=swept.at[pl.ds(group * GROUP, GROUP), pl.ds(0, 2)],
            dst_ref=from_north.at[group],
            send_sem=send_south.at[group],
            recv_sem=recv_north.at[group],
            device_id=(tile - 1, spec),
            device_id_type=MESH,
        )

    def sweep_row(index, row):
        ratio = swept[index, row]
        for step in range(STEPS):
            flux = coef[row, step, 0]
            fore = east(ratio) - ratio
            slope = half_slope(west(fore), fore)
            eastward = flux > 0
            value = jnp.where(eastward, west(ratio), ratio) + coef[row, step, 1] * jnp.where(
                eastward, west(slope), slope
            )
            carried = flux * value
            ratio = (coef[row, step, 2] * ratio + carried - east(carried)) * coef[row, step, 3]
        swept[index, row] = ratio

    def zonal_group(group, carry):
        def one_row(row, inner):
            for k in range(GROUP):
                sweep_row(group * GROUP + k, row)
            return inner

        lax.fori_loop(0, ROWS, one_row, 0)
        pl.when(has_north)(lambda: up(group).start())
        pl.when(has_south)(lambda: down(group).start())
        return carry

    lax.fori_loop(0, groups, zonal_group, 0)

    @pl.when(has_south)
    def _():
        edge_down().wait_send()
        edge_up().wait_recv()

    @pl.when(has_north)
    def _():
        edge_up().wait_send()
        edge_down().wait_recv()

    @pl.when(jnp.logical_not(has_south))
    def _():
        got_south[0] = last_mass[0]

    @pl.when(jnp.logical_not(has_north))
    def _():
        got_north[0] = last_mass[ROWS - 1]
        got_north[1] = jnp.zeros((COLS, LEVELS, LANES), jnp.float32)

    def row_mass(row):
        if row < 0:
            return got_south[0]
        return last_mass[row] if row < ROWS else got_north[0]

    def face_flux(face):
        if face == 0:
            return jnp.where(has_south, field[2, 0], 0.0)
        return field[2, face] if face < ROWS else got_north[1]

    for face in range(ROWS + 1):
        flux = face_flux(face)
        faces[face, 0] = flux
        faces[face, 1] = jnp.where(
            flux > 0, 1.0 - flux / row_mass(face - 1), -1.0 - flux / row_mass(face)
        )
    for row in range(ROWS):
        mass = row_mass(row) + faces[row, 0] - faces[row + 1, 0]
        cells[row, 0] = row_mass(row)
        cells[row, 1] = 1.0 / mass
        masses_new[row] = mass
    masses_new[ROWS:] = jnp.zeros((PACK - ROWS, COLS, LEVELS, LANES), jnp.float32)

    def turn_out(read, write):
        for col in range(COLS):
            back_turned[pl.ds(col, LANES, stride=COLS), :] = read(col).reshape(LANES, LANES).T
        for col in range(COLS):
            lanes = slice(col * LANES, min((col + 1) * LANES, NX))
            width = lanes.stop - lanes.start
            write(lanes, back_turned[lanes, :].T.reshape(PACK, LEVELS, width))

    def write_mass(lanes, value):
        mass_out[:, :, lanes] = value[:ROWS]

    turn_out(lambda col: masses_new[:, col], write_mass)

    def merid_part(group, k, col):
        index = group * GROUP + k
        rows = [from_south[group, k, j, col] for j in range(2)]
        rows += [swept[index, row, col] for row in range(ROWS)]
        rows += [from_north[group, k, j, col] for j in range(2)]
        diffs = [rows[j + 1] - rows[j] for j in range(ROWS + 3)]
        slopes = [half_slope(diffs[j], diffs[j + 1]) for j in range(ROWS + 2)]
        carried = []
        for face in range(ROWS + 1):
            flux = faces[face, 0, col]
            northward = flux > 0
            value = jnp.where(northward, rows[face + 1], rows[face + 2]) + faces[
                face, 1, col
            ] * jnp.where(northward, slopes[face], slopes[face + 1])
            carried.append(flux * value)
        for row in range(ROWS):
            swept[index, row, col] = (
                cells[row, 0, col] * rows[row + 2] + carried[row] - carried[row + 1]
            ) * cells[row, 1, col]

    def merid_group(group, carry):
        @pl.when(has_south)
        def _():
            up(group).wait_recv()
            down(group).wait_send()

        @pl.when(has_north)
        def _():
            down(group).wait_recv()
            up(group).wait_send()

        for k in range(GROUP):

            @pl.when(jnp.logical_not(has_south))
            def _():
                for j in range(2):
                    from_south[group, k, j] = swept[group * GROUP + k, 0]

            @pl.when(jnp.logical_not(has_north))
            def _():
                for j in range(2):
                    from_north[group, k, j] = swept[group * GROUP + k, ROWS - 1]

        def block(col, inner):
            for k in range(GROUP):
                merid_part(group, k, col)
            return inner

        lax.fori_loop(0, COLS, block, 0)
        return carry

    def finish(pack, carry):
        each = PACK // GROUP
        lax.fori_loop(pack * each, (pack + 1) * each, merid_group, 0)
        part = pl.ds(pack * PACK, PACK)

        def one(row, inner):
            def write(lanes, value):
                out[part, row, :, lanes] = value

            turn_out(lambda col: swept[part, row, col], write)
            return inner

        lax.fori_loop(0, ROWS, one, 0)
        return carry

    lax.fori_loop(0, packs, finish, 0)


def shards(tiles, tracer, air_mass, zonal_flux, meridional_flux, substeps):
    species = tracer.shape[0]
    groups = species // GROUP
    rows_first = [jnp.transpose(x, (1, 0, 2)) for x in (air_mass, zonal_flux, meridional_flux)]
    f32 = jnp.float32
    dma = pltpu.SemaphoreType.DMA

    def body(*refs):
        kernel(tiles, *refs)

    def rows(*lead):
        return pltpu.VMEM((*lead, COLS, LEVELS, LANES), f32)

    vmem = pl.BlockSpec(memory_space=pltpu.VMEM)
    ratios, masses = pl.pallas_call(
        body,
        out_shape=(
            pltpu.VMEM((species, ROWS, LEVELS, NX), f32),
            pltpu.VMEM((ROWS, LEVELS, NX), f32),
        ),
        in_specs=[
            pl.BlockSpec(memory_space=pl.ANY),
            vmem,
            vmem,
            vmem,
            pl.BlockSpec(memory_space=pltpu.SMEM),
        ],
        out_specs=(vmem, vmem),
        scratch_shapes=[
            rows(species, ROWS),
            pltpu.VMEM((WIDE, LANES), f32),
            pltpu.VMEM((WIDE, LANES), f32),
            pltpu.VMEM((WIDE, LANES), f32),
            pltpu.VMEM((FIELD_ROWS, NX), f32),
            pltpu.VMEM((LEVELS, FIELD_ROWS, NX), f32),
            pltpu.VMEM((COLS, LEVELS * FIELD_ROWS, LANES), f32),
            rows(3, ROWS),
            rows(ROWS, STEPS, 4),
            rows(ROWS),
            rows(groups, GROUP, 2),
            rows(groups, GROUP, 2),
            rows(2),
            rows(1),
            rows(1),
            rows(2),
            rows(ROWS + 1, 2),
            rows(ROWS, 2),
            rows(PACK),
            dma((species // PACK * ROWS,)),
            dma((LEVELS,)),
            dma((LEVELS,)),
            dma((groups,)),
            dma((groups,)),
            dma((groups,)),
            dma((groups,)),
            dma((2,)),
            dma((2,)),
        ],
        compiler_params=pltpu.CompilerParams(
            collective_id=0, has_side_effects=True, vmem_limit_bytes=50 * 2**20
        ),
        cost_estimate=pl.CostEstimate(flops=10**9, bytes_accessed=2 * 10**7, transcendentals=0),
    )(jnp.transpose(tracer, (0, 2, 1, 3)), *rows_first, substeps)
    return jnp.transpose(ratios, (0, 2, 1, 3)), jnp.transpose(masses, (1, 0, 2))


def solution(mesh):
    tiles = mesh.shape["tile"]

    def run(*args):
        return shards(tiles, *args)

    placed = (
        P("spec", None, "tile", None),
        P("spec", "tile", None),
        P("spec", "tile", None),
        P("spec", "tile", None),
        P(),
    )
    return jax.shard_map(
        run,
        mesh=mesh,
        in_specs=placed,
        out_specs=(P("spec", None, "tile", None), P(None, "tile", None)),
        check_vma=False,
    )
```

time: 167 us -> 109 us (0.65)
  Pallas kernels: 157 us -> 103 us
  local copies, waits for them, and re-layouts: 9.56 us -> 4.46 us
    pallas_call x1, Pallas kernels: 157 us -> 103 us  [shards(): pl.pallas_call(body, out_shape=(pltpu.VMEM((species, ROWS, LEVELS, NX), f...]
    unnamed x4 -> x2, local copies, waits for them, and re-layouts: 9.56 us -> 4.46 us
where the time goes in v2:
time: 109 us; the launch traced here: 108 us
  Pallas kernels  103 us (94%)
  local copies, waits for them, and re-layouts  4.46 us (4%)
    pallas_call x1, Pallas kernels, shards(): pl.pallas_call(body, out_shape=(pltpu.VMEM((species, ROWS, LEVELS, NX), f...  103 us
    unnamed x2, local copies, waits for them, and re-layouts  4.46 us

profile of v2, /device:TPU:1, one launch (start us, length us, event | category | flops | bytes accessed | tf_op | source)
XLA Modules:
  0.0 108.2 jit_solution(8659601881529907374)
XLA Ops:
  0.6 103.1 %shard_map.68 = (f32[32,6,8,1440]{3,2,1,0:T(8,128)S(1)}, f32[6,8,1440]{2,1,0:T(8,128)S(1)}) custom-call(f32[32,6,8,1440]{3,2,1,0:T(8,128)} %bitcast.8, f32[6,1,1440]{2,1,0:T(1,128)} %bitcast.9, f32[6,1,1440]{2,1,0:T(1,128)} %bitcast.10, f32[6,1,1440]{2,1,0:T(1,128)} %bitcast.11, s32[96]{0:T(128)} %refs_4_.1), custom_call_target="tpu_custom_call" | custom-call | flops 1000000000 | bytes 20000000 | tf_op jit(solution)/shard_map/pallas_call | solution.py:434
  103.7 3.7 %copy.9 = f32[32,8,6,1440]{3,1,2,0:T(8,128)} copy(f32[32,8,6,1440]{3,1,2,0:T(8,128)S(1)} %bitcast.6) | data formatting | bytes 17694720
  107.5 0.7 copy.10

commit v3 on v2

v3 whole, which is shorter than its diff:
```python
import jax
import jax.numpy as jnp
from jax import lax
from jax.experimental import pallas as pl
from jax.experimental.pallas import tpu as pltpu
from jax.sharding import PartitionSpec as P

MESH = pl.DeviceIdType.MESH
NX = 1440
LANES = 128
COLS = 12
WIDE = COLS * LANES
LEVELS = 8
ROWS = 6
STEPS = 4
GROUP = 8
PIECE = 2
EACH = GROUP // PIECE
PACK = LANES // LEVELS
FIRST_ROWS = 16
FULL = NX // LANES


def east(value):
    return jnp.concatenate([value[1:], pltpu.roll(value[0], LANES - 1, 1)[None]], axis=0)


def west(value):
    return jnp.concatenate([pltpu.roll(value[COLS - 1], 1, 1)[None], value[: COLS - 1]], axis=0)


def half_slope(back, fore):
    low = jnp.maximum(jnp.minimum(back, fore), 0.0)
    high = jnp.minimum(jnp.maximum(back, fore), 0.0)
    return jnp.maximum(jnp.minimum(0.25 * (back + fore), low), high)


def wrap(turned):
    turned[NX : NX + COLS, :] = turned[0:COLS, :]
    turned[WIDE - COLS : WIDE, :] = turned[NX - COLS : NX, :]


def every(turned, col):
    return turned[pl.ds(col, LANES, stride=COLS), :]


def kernel(
    tiles,
    tracer,
    air,
    zonal,
    merid,
    substeps,
    out,
    mass_out,
    swept,
    turned,
    turned_more,
    back_turned,
    mine,
    mine_more,
    gathered,
    gathered_more,
    levels,
    levels_more,
    field,
    coef,
    last_mass,
    raw,
    outer,
    inner,
    kept_flux,
    kept_slope,
    edge_outer,
    edge_inner,
    got_outer,
    got_inner,
    faces,
    cells,
    masses_new,
    load_sem,
    gather_send,
    gather_recv,
    more_send,
    more_recv,
    outer_send,
    outer_recv,
    inner_send,
    inner_recv,
    edge_send,
    edge_recv,
):
    tile = lax.axis_index("tile")
    spec = lax.axis_index("spec")
    species = tracer.shape[0]
    groups = species // GROUP
    packs = species // PACK
    odd = lax.rem(tile, 2)
    is_odd = odd == 1
    outer_tile = tile + 2 * odd - 1
    inner_tile = tile + 1 - 2 * odd
    has_outer = jnp.logical_and(tile > 0, tile < tiles - 1)

    def place(row):
        return row + odd * (ROWS - 1 - 2 * row)

    def load(pack, row):
        part = pl.ds(pack * PACK, PACK)
        return pltpu.make_async_copy(
            tracer.at[part, row], out.at[part, row], load_sem.at[pack * ROWS + row]
        )

    def start_load(index, carry):
        load(lax.rem(index, packs), place(index // packs)).start()
        return carry

    lax.fori_loop(0, packs * ROWS, start_load, 0)

    half = LEVELS // 2
    partner = lax.rem(spec + half, LEVELS)
    side = (spec // half) * half
    peers = [side + lax.rem(spec + step, half) for step in range(1, half)]

    barrier = pltpu.get_barrier_semaphore()
    for peer in [partner] + peers:
        pl.semaphore_signal(barrier, inc=1, device_id=(tile, peer), device_id_type=MESH)
    pl.semaphore_signal(barrier, inc=1, device_id=(inner_tile, spec), device_id_type=MESH)

    @pl.when(has_outer)
    def _():
        pl.semaphore_signal(barrier, inc=1, device_id=(outer_tile, spec), device_id_type=MESH)

    mine[2 * ROWS :, :] = jnp.zeros((FIRST_ROWS - 2 * ROWS, NX), jnp.float32)
    mine_more[ROWS:, :] = jnp.zeros((LEVELS - ROWS, NX), jnp.float32)
    for row in range(ROWS):
        mine[row : row + 1, :] = air[place(row)]
        mine[ROWS + row : ROWS + row + 1, :] = zonal[place(row)]
        mine_more[row : row + 1, :] = merid[place(row)]
    gathered[spec] = mine[...]
    gathered_more[spec] = mine_more[...]

    greeted = half + 1 + has_outer.astype(jnp.int32)
    pl.semaphore_wait(barrier, greeted)

    first_kind = (mine, gathered, gather_send, gather_recv)
    more_kind = (mine_more, gathered_more, more_send, more_recv)

    def give(kind, level, peer, slot, source=None):
        own, target, send, recv = kind
        return pltpu.make_async_remote_copy(
            src_ref=own if source is None else source,
            dst_ref=target.at[level],
            send_sem=send.at[slot],
            recv_sem=recv.at[level],
            device_id=(tile, peer),
            device_id_type=MESH,
        )

    def give_own(kind):
        give(kind, spec, partner, 0).start()
        for k, peer in enumerate(peers):
            give(kind, spec, peer, 1 + k).start()

    def pass_on(kind):
        give(kind, partner, partner, 0).wait()
        for k, peer in enumerate(peers):
            give(kind, partner, peer, half + k, kind[1].at[partner]).start()

    def settle(kind):
        for k, peer in enumerate(peers):
            give(kind, spec, peer, 1 + k).wait_send()
            give(kind, partner, peer, half + k, kind[1].at[partner]).wait_send()
        for step in range(1, half):
            level = side + lax.rem(spec + half - step, half)
            for got in (level, lax.rem(level + half, LEVELS)):
                give(kind, got, partner, 0).wait_recv()

    def across(piece):
        part = pl.ds(piece * PIECE, PIECE)
        return pltpu.make_async_remote_copy(
            src_ref=out.at[part, pl.ds(odd * (ROWS - 2), 2)],
            dst_ref=raw.at[part],
            send_sem=outer_send.at[piece],
            recv_sem=outer_recv.at[piece],
            device_id=(outer_tile, spec),
            device_id_type=MESH,
        )

    def send_across(piece, due=True):
        @pl.when(jnp.logical_and(has_outer, due))
        def _():
            across(piece).start()

    give_own(first_kind)
    for row in range(2):
        for pack in range(packs):
            load(pack, place(row)).wait()

    give_own(more_kind)
    pass_on(first_kind)
    pass_on(more_kind)

    for piece in range(3):
        send_across(piece)

    for buffer in (turned, turned_more):
        buffer[NX:WIDE, :] = jnp.ones((WIDE - NX, LANES), jnp.float32)

    def turn_in(read, write, count):
        wide = count * LEVELS
        for col in range(COLS):
            lanes = slice(col * LANES, min((col + 1) * LANES, NX))
            width = lanes.stop - lanes.start
            turned[lanes, 0:wide] = read(lanes).reshape(wide, width).T
        wrap(turned)
        for col in range(COLS):
            write(col, every(turned, col).T[:wide].reshape(count, LEVELS, LANES))

    def turn_own(pack, row):
        part = pl.ds(pack * PACK, PACK)

        @pl.when(row >= 2)
        def _():
            load(pack, place(row)).wait()


        def write(col, value):
            swept[part, row, col] = value

        turn_in(lambda lanes: out[part, place(row), :, lanes], write, PACK)

    def turn_one(index, carry):
        send_across(3 + index // ROWS, lax.rem(index, ROWS) == ROWS - 2)
        turn_own(index // ROWS, lax.rem(index, ROWS))
        return carry

    lax.fori_loop(0, packs * ROWS, turn_one, 0)
    settle(first_kind)

    def turn_fields(source, level_ref, rows):
        wide = LEVELS * rows
        for col in range(COLS):
            lanes = slice(col * LANES, min((col + 1) * LANES, NX))
            width = lanes.stop - lanes.start
            turned_more[lanes, 0:wide] = source[:, :, lanes].reshape(wide, width).T
        wrap(turned_more)
        for col in range(COLS):
            level_ref[col] = every(turned_more, col).T[:wide]

    turn_fields(gathered, levels, FIRST_ROWS)
    for col in range(COLS):
        for index in range(2):
            for row in range(ROWS):
                field[index, row, col] = levels[
                    col, pl.ds(index * ROWS + row, LEVELS, stride=FIRST_ROWS), :
                ]

    first = tile * ROWS

    def prepare(slot, place_of, mass, share):
        count = substeps[place_of]
        share = share / count.astype(jnp.float32)
        for step in range(STEPS):
            flux = jnp.where(step < count, share, 0.0)
            coef[slot, step, 0] = flux
            coef[slot, step, 1] = jnp.where(flux > 0, 1.0 - flux / west(mass), -1.0 - flux / mass)
            coef[slot, step, 2] = mass
            mass = mass + flux - east(flux)
            coef[slot, step, 3] = 1.0 / mass
        last_mass[slot] = mass

    def prepare_own(row, carry):
        prepare(row, first + place(row), field[0, row], field[1, row])
        return carry

    lax.fori_loop(0, ROWS, prepare_own, 0)

    def sweep(ref, group, row, slot):
        for k in range(GROUP):
            index = group * GROUP + k
            ratio = ref[index, row]
            for step in range(STEPS):
                flux = coef[slot, step, 0]
                fore = east(ratio) - ratio
                slope = half_slope(west(fore), fore)
                eastward = flux > 0
                value = jnp.where(eastward, west(ratio), ratio) + coef[slot, step, 1] * jnp.where(
                    eastward, west(slope), slope
                )
                carried = flux * value
                ratio = (coef[slot, step, 2] * ratio + carried - east(carried)) * coef[
                    slot, step, 3
                ]
            ref[index, row] = ratio

    def beside(group):
        part = pl.ds(group * GROUP, GROUP)
        return pltpu.make_async_remote_copy(
            src_ref=swept.at[part, pl.ds(ROWS - 2, 2)],
            dst_ref=inner.at[part],
            send_sem=inner_send.at[group],
            recv_sem=inner_recv.at[group],
            device_id=(inner_tile, spec),
            device_id_type=MESH,
        )

    send_across(5)

    def sweep_inner(group, carry):
        send_across(6 + group // 2, lax.rem(group, 2) == 0)

        def one(row, inside):
            sweep(swept, group, ROWS - 2 + row, ROWS - 2 + row)
            return inside

        lax.fori_loop(0, 2, one, 0)
        beside(group).start()
        return carry

    lax.fori_loop(0, groups, sweep_inner, 0)

    settle(more_kind)
    turn_fields(gathered_more, levels_more, LEVELS)
    for col in range(COLS):
        for row in range(ROWS):
            field[2, row, col] = levels_more[col, pl.ds(row, LEVELS, stride=LEVELS), :]

    for index in range(2):
        for row in range(2):
            edge_outer[2 * index + row] = field[index, row]
    edge_outer[4] = field[2, 0]
    edge_inner[0] = last_mass[ROWS - 1]
    edge_inner[1] = field[2, ROWS - 1]

    def edge(index):
        return pltpu.make_async_remote_copy(
            src_ref=(edge_outer, edge_inner)[index],
            dst_ref=(got_outer, got_inner)[index],
            send_sem=edge_send.at[index],
            recv_sem=edge_recv.at[index],
            device_id=((outer_tile, inner_tile)[index], spec),
            device_id_type=MESH,
        )

    edge(1).start()
    pl.when(has_outer)(lambda: edge(0).start())

    def sweep_rest(index, carry):
        send_across(8 + index // 4, lax.rem(index, 4) == 0)
        sweep(swept, lax.rem(index, groups), index // groups, index // groups)
        return carry

    lax.fori_loop(0, groups * (ROWS - 2), sweep_rest, 0)

    edge(1).wait()

    def row_mass(row):
        if row < 0:
            return last_mass[ROWS]
        return last_mass[row] if row < ROWS else got_inner[0]

    def own_flux(row):
        if row < 0:
            return got_outer[4]
        return field[2, row] if row < ROWS else got_inner[1]

    def make_face(face):
        flux = jnp.where(is_odd, -own_flux(face - 1), own_flux(face))
        if face == 0:
            flux = jnp.where(has_outer, flux, 0.0)
        faces[face, 0] = flux
        faces[face, 1] = jnp.where(
            flux > 0, 1.0 - flux / row_mass(face - 1), -1.0 - flux / row_mass(face)
        )

    def make_cell(row):
        mass = row_mass(row) + faces[row, 0] - faces[row + 1, 0]
        cells[row, 0] = row_mass(row)
        cells[row, 1] = 1.0 / mass
        masses_new[row] = mass

    for face in range(1, ROWS + 1):
        make_face(face)
    for row in range(1, ROWS):
        make_cell(row)
    masses_new[ROWS:] = jnp.zeros((PACK - ROWS, COLS, LEVELS, LANES), jnp.float32)

    def turn_out(read, write, count):
        wide = count * LEVELS
        for col in range(COLS):
            back_turned[pl.ds(col, LANES, stride=COLS), 0:wide] = read(col).reshape(wide, LANES).T
        for col in range(COLS):
            lanes = slice(col * LANES, min((col + 1) * LANES, NX))
            width = lanes.stop - lanes.start
            write(lanes, back_turned[lanes, :].T[:wide].reshape(count, LEVELS, width))

    def write_mass(lanes, value):
        for row in range(ROWS):
            mass_out[place(row), :, lanes] = value[row]

    def through(face, col, near, far, near_slope, far_slope):
        flux = faces[face, 0, col]
        onward = flux > 0
        value = jnp.where(onward, near, far) + faces[face, 1, col] * jnp.where(
            onward, near_slope, far_slope
        )
        return flux * value

    def renewed(row, col, ratio, enters, leaves):
        return (cells[row, 0, col] * ratio + enters - leaves) * cells[row, 1, col]

    def merid_far(index, col):
        rows = [swept[index, row, col] for row in range(ROWS)]
        rows += [inner[index, 1, col], inner[index, 0, col]]
        diffs = [rows[j + 1] - rows[j] for j in range(ROWS + 1)]
        slopes = [None] + [half_slope(diffs[j - 1], diffs[j]) for j in range(1, ROWS + 1)]
        carried = {
            face: through(
                face, col, rows[face - 1], rows[face], slopes[face - 1], slopes[face]
            )
            for face in range(2, ROWS + 1)
        }
        kept_flux[index, col] = carried[2]
        kept_slope[index, col] = slopes[1]
        for row in range(2, ROWS):
            swept[index, row, col] = renewed(row, col, rows[row], carried[row], carried[row + 1])

    def merid_near(index, col):
        rows = [outer[index, 1, col], outer[index, 0, col]]
        rows += [swept[index, row, col] for row in range(2)]
        diffs = [rows[j + 1] - rows[j] for j in range(3)]
        slopes = [half_slope(diffs[j], diffs[j + 1]) for j in range(2)]
        slopes.append(kept_slope[index, col])
        first_flux = through(0, col, rows[1], rows[2], slopes[0], slopes[1])
        second_flux = through(1, col, rows[2], rows[3], slopes[1], slopes[2])
        swept[index, 0, col] = renewed(0, col, rows[2], first_flux, second_flux)
        swept[index, 1, col] = renewed(1, col, rows[3], second_flux, kept_flux[index, col])

    def write_out(part, row):
        def write(lanes, value):
            out[part, place(row), :, lanes] = value

        return write

    def merid_all(group, work, pairs):
        def block(index, carry):
            col = lax.rem(index, COLS)
            for k in range(pairs):
                work(group * GROUP + (index // COLS) * pairs + k, col)
            return carry

        lax.fori_loop(0, COLS * (GROUP // pairs), block, 0)

    def far_group(group, carry):
        send_across(12 + group // 2, lax.rem(group, 2) == 0)
        beside(group).wait()
        merid_all(group, merid_far, 2)
        return carry

    lax.fori_loop(0, groups, far_group, 0)

    def far_out(index, carry):
        send_across(14 + index // 4, lax.rem(index, 4) == 0)
        part = pl.ds((index // (ROWS - 2)) * PACK, PACK)
        row = 2 + lax.rem(index, ROWS - 2)
        turn_out(lambda col: swept[part, row, col], write_out(part, row), PACK)
        return carry

    lax.fori_loop(0, packs * (ROWS - 2), far_out, 0)

    pl.when(has_outer)(lambda: edge(0).wait())

    @pl.when(jnp.logical_not(has_outer))
    def _():
        for row in range(2):
            got_outer[row] = field[0, row]
            got_outer[2 + row] = field[1, row]
        got_outer[4] = jnp.zeros((COLS, LEVELS, LANES), jnp.float32)

    def prepare_outer(row, carry):
        there = first + (1 - odd) * (-1 - row) + odd * (ROWS + row)
        there = jnp.where(has_outer, there, first + place(0))
        prepare(ROWS + row, there, got_outer[row], got_outer[2 + row])
        return carry

    lax.fori_loop(0, 2, prepare_outer, 0)

    make_face(0)
    make_cell(0)
    turn_out(lambda col: masses_new[:, col], write_mass, PACK)

    def near_row(row):
        return odd * row + (1 - odd) * (1 - row)

    def near_group(group, carry):
        part = pl.ds(group * GROUP, GROUP)

        @pl.when(has_outer)
        def _():
            def arrive(k, inside):
                across(group * EACH + k).wait()
                return inside

            lax.fori_loop(0, EACH, arrive, 0)

            def one(row, inside):
                def write(col, value):
                    outer[part, row, col] = value

                turn_in(lambda lanes: raw[part, near_row(row), :, lanes], write, GROUP)
                sweep(outer, group, row, ROWS + row)
                return inside

            lax.fori_loop(0, 2, one, 0)

        @pl.when(jnp.logical_not(has_outer))
        def _():
            def same(k, inside):
                for row in range(2):
                    outer[group * GROUP + k, row] = swept[group * GROUP + k, 0]
                return inside

            lax.fori_loop(0, GROUP, same, 0)

        merid_all(group, merid_near, 4)

        def back(row, inside):
            turn_out(lambda col: swept[part, row, col], write_out(part, row), GROUP)
            return inside

        lax.fori_loop(0, 2, back, 0)
        return carry

    lax.fori_loop(0, groups, near_group, 0)


def shards(tiles, tracer, air_mass, zonal_flux, meridional_flux, substeps):
    species = tracer.shape[0]
    groups = species // GROUP
    rows_first = [jnp.transpose(x, (1, 0, 2)) for x in (air_mass, zonal_flux, meridional_flux)]
    f32 = jnp.float32
    dma = pltpu.SemaphoreType.DMA

    def body(*refs):
        kernel(tiles, *refs)

    def rows(*lead):
        return pltpu.VMEM((*lead, COLS, LEVELS, LANES), f32)

    vmem = pl.BlockSpec(memory_space=pltpu.VMEM)
    ratios, masses = pl.pallas_call(
        body,
        out_shape=(
            pltpu.VMEM((species, ROWS, LEVELS, NX), f32),
            pltpu.VMEM((ROWS, LEVELS, NX), f32),
        ),
        in_specs=[
            pl.BlockSpec(memory_space=pl.ANY),
            vmem,
            vmem,
            vmem,
            pl.BlockSpec(memory_space=pltpu.SMEM),
        ],
        out_specs=(vmem, vmem),
        scratch_shapes=[
            rows(species, ROWS),
            pltpu.VMEM((WIDE, LANES), f32),
            pltpu.VMEM((WIDE, LANES), f32),
            pltpu.VMEM((WIDE, LANES), f32),
            pltpu.VMEM((FIRST_ROWS, NX), f32),
            pltpu.VMEM((LEVELS, NX), f32),
            pltpu.VMEM((LEVELS, FIRST_ROWS, NX), f32),
            pltpu.VMEM((LEVELS, LEVELS, NX), f32),
            pltpu.VMEM((COLS, LEVELS * FIRST_ROWS, LANES), f32),
            pltpu.VMEM((COLS, LEVELS * LEVELS, LANES), f32),
            rows(3, ROWS),
            rows(ROWS + 2, STEPS, 4),
            rows(ROWS + 2),
            pltpu.VMEM((species, 2, LEVELS, NX), f32),
            rows(species, 2),
            rows(species, 2),
            rows(species),
            rows(species),
            rows(5),
            rows(2),
            rows(5),
            rows(2),
            rows(ROWS + 1, 2),
            rows(ROWS, 2),
            rows(PACK),
            dma((species // PACK * ROWS,)),
            dma((LEVELS,)),
            dma((LEVELS,)),
            dma((LEVELS,)),
            dma((LEVELS,)),
            dma((species // PIECE,)),
            dma((species // PIECE,)),
            dma((groups,)),
            dma((groups,)),
            dma((2,)),
            dma((2,)),
        ],
        compiler_params=pltpu.CompilerParams(
            collective_id=0, has_side_effects=True, vmem_limit_bytes=50 * 2**20
        ),
        cost_estimate=pl.CostEstimate(flops=10**9, bytes_accessed=2 * 10**7, transcendentals=0),
    )(jnp.transpose(tracer, (0, 2, 1, 3)), *rows_first, substeps)
    return jnp.transpose(ratios, (0, 2, 1, 3)), jnp.transpose(masses, (1, 0, 2))


def solution(mesh):
    tiles = mesh.shape["tile"]

    def run(*args):
        return shards(tiles, *args)

    placed = (
        P("spec", None, "tile", None),
        P("spec", "tile", None),
        P("spec", "tile", None),
        P("spec", "tile", None),
        P(),
    )
    return jax.shard_map(
        run,
        mesh=mesh,
        in_specs=placed,
        out_specs=(P("spec", None, "tile", None), P(None, "tile", None)),
        check_vma=False,
    )
```

time: 109 us -> 97.3 us (0.89)
  Pallas kernels: 103 us -> 91.9 us
    pallas_call x1, Pallas kernels: 103 us -> 91.9 us  [shards(): pl.pallas_call(body, out_shape=(pltpu.VMEM((species, ROWS, LEVELS, NX), f...]
where the time goes in v3:
time: 97.3 us; the launch traced here: 97 us
  Pallas kernels  91.9 us (94%)
  local copies, waits for them, and re-layouts  4.46 us (5%)
    pallas_call x1, Pallas kernels, shards(): pl.pallas_call(body, out_shape=(pltpu.VMEM((species, ROWS, LEVELS, NX), f...  91.9 us
    unnamed x2, local copies, waits for them, and re-layouts  4.46 us

profile of v3, /device:TPU:1, one launch (start us, length us, event | category | flops | bytes accessed | tf_op | source)
XLA Modules:
  0.0 97.0 jit_solution(8799560189866867157)
XLA Ops:
  0.6 91.9 %shard_map.68 = (f32[32,6,8,1440]{3,2,1,0:T(8,128)S(1)}, f32[6,8,1440]{2,1,0:T(8,128)S(1)}) custom-call(f32[32,6,8,1440]{3,2,1,0:T(8,128)} %bitcast.8, f32[6,1,1440]{2,1,0:T(1,128)} %bitcast.9, f32[6,1,1440]{2,1,0:T(1,128)} %bitcast.10, f32[6,1,1440]{2,1,0:T(1,128)} %bitcast.11, s32[96]{0:T(128)} %refs_4_.1), custom_call_target="tpu_custom_call" | custom-call | flops 1000000000 | bytes 20000000 | tf_op jit(solution)/shard_map/pallas_call | solution.py:551
  92.6 3.7 %copy.9 = f32[32,8,6,1440]{3,1,2,0:T(8,128)} copy(f32[32,8,6,1440]{3,1,2,0:T(8,128)S(1)} %bitcast.6) | data formatting | bytes 17694720
  96.3 0.7 copy.10

commit v4 on v3

--- a/solution.py
+++ b/solution.py
@@ -16,6 +16,16 @@
 GROUP = 8
 PIECE = 2
 EACH = GROUP // PIECE
+RAW_GROUPS = 2
+RAW_PIECES = RAW_GROUPS * EACH
+WHOLE = NX // LANES * LANES
+REST = NX - WHOLE
+SHARE = LANES // REST
+USED = NX // COLS
+SPARE = LANES - USED
+SLOTS = USED // SPARE
+ROW_SETS = PIECE * 2
+DENSE = ROW_SETS * COLS * USED // LANES
 PACK = LANES // LEVELS
 FIRST_ROWS = 16
 FULL = NX // LANES
@@ -67,6 +77,10 @@
     coef,
     last_mass,
     raw,
+    rests,
+    got_rests,
+    dense,
+    got_dense,
     outer,
     inner,
     kept_flux,
@@ -175,43 +189,118 @@
             for got in (level, lax.rem(level + half, LEVELS)):
                 give(kind, got, partner, 0).wait_recv()
 
-    def across(piece):
+    def across(piece, swept_already):
         part = pl.ds(piece * PIECE, PIECE)
+        if swept_already:
+            source, target = dense.at[piece - RAW_PIECES], got_dense.at[piece - RAW_PIECES]
+        else:
+            lanes = pl.ds(0, WHOLE)
+            source = out.at[part, pl.ds(odd * (ROWS - 2), 2), :, lanes]
+            target = raw.at[part]
         return pltpu.make_async_remote_copy(
-            src_ref=out.at[part, pl.ds(odd * (ROWS - 2), 2)],
-            dst_ref=raw.at[part],
+            src_ref=source,
+            dst_ref=target,
             send_sem=outer_send.at[piece],
             recv_sem=outer_recv.at[piece],
             device_id=(outer_tile, spec),
             device_id_type=MESH,
         )
 
-    def send_across(piece, due=True):
+    def rest_across():
+        return pltpu.make_async_remote_copy(
+            src_ref=rests,
+            dst_ref=got_rests,
+            send_sem=edge_send.at[2],
+            recv_sem=edge_recv.at[2],
+            device_id=(outer_tile, spec),
+            device_id_type=MESH,
+        )
+
+    lane = lax.broadcasted_iota(jnp.int32, (LEVELS, LANES), 1)
+
+    def spot(index):
+        return index // (2 * COLS), (index // COLS) % 2, index % COLS
+
+    def pack_piece(piece):
+        for index in range(DENSE):
+            k, row, col = spot(index)
+            value = swept[piece * PIECE + k, row, col]
+            k, row, col = spot(DENSE + index // SLOTS)
+            moved = pltpu.roll(
+                swept[piece * PIECE + k, row, col], USED - SPARE * (index % SLOTS), 1
+            )
+            dense[piece - RAW_PIECES, index] = jnp.where(lane < USED, value, moved)
+
+    def unpack_piece(piece):
+        for index in range(DENSE):
+            k, row, col = spot(index)
+            outer[piece * PIECE + k, row, col] = got_dense[piece - RAW_PIECES, index]
+        for last in range(ROW_SETS * COLS - DENSE):
+            value = got_dense[piece - RAW_PIECES, last * SLOTS + SLOTS - 1]
+            value = pltpu.roll(value, SPARE * (SLOTS - 1) + LANES - USED, 1)
+            for slot in range(SLOTS - 1):
+                moved = pltpu.roll(
+                    got_dense[piece - RAW_PIECES, last * SLOTS + slot],
+                    SPARE * slot + LANES - USED,
+                    1,
+                )
+                inside = jnp.logical_and(lane >= SPARE * slot, lane < SPARE * (slot + 1))
+                value = jnp.where(inside, moved, value)
+            k, row, col = spot(DENSE + last)
+            outer[piece * PIECE + k, row, col] = value
+
+    def send_across(piece, swept_already, due=True):
         @pl.when(jnp.logical_and(has_outer, due))
         def _():
-            across(piece).start()
+            if swept_already:
+                pack_piece(piece)
+            across(piece, swept_already).start()
 
     give_own(first_kind)
     for row in range(2):
         for pack in range(packs):
             load(pack, place(row)).wait()
 
+    for group in range(RAW_GROUPS):
+        for row in range(2):
+            for k in range(GROUP // SHARE):
+                rests[group, row, k] = jnp.concatenate(
+                    [
+                        out[
+                            group * GROUP + j * (GROUP // SHARE) + k,
+                            odd * (ROWS - 2) + row,
+                            :,
+                            WHOLE:NX,
+                        ]
+                        for j in range(SHARE)
+                    ],
+                    axis=1,
+                )
+
     give_own(more_kind)
+    for piece in range(1):
+        send_across(piece, False)
     pass_on(first_kind)
     pass_on(more_kind)
 
-    for piece in range(3):
-        send_across(piece)
+    for piece in range(1, 3):
+        send_across(piece, False)
+    pl.when(has_outer)(lambda: rest_across().start())
 
     for buffer in (turned, turned_more):
         buffer[NX:WIDE, :] = jnp.ones((WIDE - NX, LANES), jnp.float32)
 
-    def turn_in(read, write, count):
+    def turn_in(read, write, count, rest=None):
         wide = count * LEVELS
-        for col in range(COLS):
+        for col in range(COLS if rest is None else FULL):
             lanes = slice(col * LANES, min((col + 1) * LANES, NX))
             width = lanes.stop - lanes.start
             turned[lanes, 0:wide] = read(lanes).reshape(wide, width).T
+        if rest is not None:
+            few = wide // SHARE
+            block = rest.reshape(few, LANES).T
+            for j in range(SHARE):
+                turned[WHOLE:NX, j * few : (j + 1) * few] = block[j * REST : (j + 1) * REST]
         wrap(turned)
         for col in range(COLS):
             write(col, every(turned, col).T[:wide].reshape(count, LEVELS, LANES))
@@ -230,7 +319,7 @@
         turn_in(lambda lanes: out[part, place(row), :, lanes], write, PACK)
 
     def turn_one(index, carry):
-        send_across(3 + index // ROWS, lax.rem(index, ROWS) == ROWS - 2)
+        send_across(3, False, index == packs * ROWS - 2)
         turn_own(index // ROWS, lax.rem(index, ROWS))
         return carry
 
@@ -304,10 +393,17 @@
             device_id_type=MESH,
         )
 
-    send_across(5)
+    send_across(4, False)
+
+    def sweep_early(index, carry):
+        row = lax.rem(index, 2)
+        sweep(swept, RAW_GROUPS + index // 2, row, row)
+        return carry
+
+    lax.fori_loop(0, 2 * (groups - RAW_GROUPS), sweep_early, 0)
 
     def sweep_inner(group, carry):
-        send_across(6 + group // 2, lax.rem(group, 2) == 0)
+        send_across(5 + group // 2, False, lax.rem(group, 2) == 0)
 
         def one(row, inside):
             sweep(swept, group, ROWS - 2 + row, ROWS - 2 + row)
@@ -345,12 +441,22 @@
     edge(1).start()
     pl.when(has_outer)(lambda: edge(0).start())
 
-    def sweep_rest(index, carry):
-        send_across(8 + index // 4, lax.rem(index, 4) == 0)
-        sweep(swept, lax.rem(index, groups), index // groups, index // groups)
-        return carry
-
-    lax.fori_loop(0, groups * (ROWS - 2), sweep_rest, 0)
+    send_across(7, False)
+
+    def sweep_middle(index, carry):
+        send_across(RAW_PIECES + index // 4, True, lax.rem(index, 4) == 0)
+        row = 2 + index // groups
+        sweep(swept, lax.rem(index, groups), row, row)
+        return carry
+
+    lax.fori_loop(0, groups * (ROWS - 4), sweep_middle, 0)
+
+    def sweep_late(index, carry):
+        row = lax.rem(index, 2)
+        sweep(swept, index // 2, row, row)
+        return carry
+
+    lax.fori_loop(0, 2 * RAW_GROUPS, sweep_late, 0)
 
     edge(1).wait()
 
@@ -452,7 +558,7 @@
         lax.fori_loop(0, COLS * (GROUP // pairs), block, 0)
 
     def far_group(group, carry):
-        send_across(12 + group // 2, lax.rem(group, 2) == 0)
+        send_across(10 + group // 2, True, lax.rem(group, 2) == 0)
         beside(group).wait()
         merid_all(group, merid_far, 2)
         return carry
@@ -460,15 +566,21 @@
     lax.fori_loop(0, groups, far_group, 0)
 
     def far_out(index, carry):
-        send_across(14 + index // 4, lax.rem(index, 4) == 0)
+        send_across(12 + index // 4, True, lax.rem(index, 4) == 0)
         part = pl.ds((index // (ROWS - 2)) * PACK, PACK)
         row = 2 + lax.rem(index, ROWS - 2)
         turn_out(lambda col: swept[part, row, col], write_out(part, row), PACK)
         return carry
 
     lax.fori_loop(0, packs * (ROWS - 2), far_out, 0)
-
-    pl.when(has_outer)(lambda: edge(0).wait())
+    for piece in (14, 15):
+        send_across(piece, True)
+
+
+    @pl.when(has_outer)
+    def _():
+        edge(0).wait()
+        rest_across().wait()
 
     @pl.when(jnp.logical_not(has_outer))
     def _():
@@ -492,13 +604,15 @@
     def near_row(row):
         return odd * row + (1 - odd) * (1 - row)
 
-    def near_group(group, carry):
+    def near_group(group, swept_already):
         part = pl.ds(group * GROUP, GROUP)
 
         @pl.when(has_outer)
         def _():
             def arrive(k, inside):
-                across(group * EACH + k).wait()
+                across(group * EACH + k, swept_already).wait()
+                if swept_already:
+                    unpack_piece(group * EACH + k)
                 return inside
 
             lax.fori_loop(0, EACH, arrive, 0)
@@ -507,11 +621,17 @@
                 def write(col, value):
                     outer[part, row, col] = value
 
-                turn_in(lambda lanes: raw[part, near_row(row), :, lanes], write, GROUP)
+                turn_in(
+                    lambda lanes: raw[part, near_row(row), :, lanes],
+                    write,
+                    GROUP,
+                    got_rests[group, near_row(row)],
+                )
                 sweep(outer, group, row, ROWS + row)
                 return inside
 
-            lax.fori_loop(0, 2, one, 0)
+            if not swept_already:
+                lax.fori_loop(0, 2, one, 0)
 
         @pl.when(jnp.logical_not(has_outer))
         def _():
@@ -529,9 +649,17 @@
             return inside
 
         lax.fori_loop(0, 2, back, 0)
-        return carry
-
-    lax.fori_loop(0, groups, near_group, 0)
+
+    def near_raw(group, carry):
+        near_group(group, False)
+        return carry
+
+    def near_swept(group, carry):
+        near_group(group, True)
+        return carry
+
+    lax.fori_loop(0, RAW_GROUPS, near_raw, 0)
+    lax.fori_loop(RAW_GROUPS, groups, near_swept, 0)
 
 
 def shards(tiles, tracer, air_mass, zonal_flux, meridional_flux, substeps):
@@ -576,7 +704,11 @@
             rows(3, ROWS),
             rows(ROWS + 2, STEPS, 4),
             rows(ROWS + 2),
-            pltpu.VMEM((species, 2, LEVELS, NX), f32),
+            pltpu.VMEM((RAW_GROUPS * GROUP, 2, LEVELS, WHOLE), f32),
+            pltpu.VMEM((RAW_GROUPS, 2, GROUP // SHARE, LEVELS, LANES), f32),
+            pltpu.VMEM((RAW_GROUPS, 2, GROUP // SHARE, LEVELS, LANES), f32),
+            pltpu.VMEM((species // PIECE - RAW_PIECES, DENSE, LEVELS, LANES), f32),
+            pltpu.VMEM((species // PIECE - RAW_PIECES, DENSE, LEVELS, LANES), f32),
             rows(species, 2),
             rows(species, 2),
             rows(species),
@@ -597,8 +729,8 @@
             dma((species // PIECE,)),
             dma((groups,)),
             dma((groups,)),
-            dma((2,)),
-            dma((2,)),
+            dma((3,)),
+            dma((3,)),
         ],
         compiler_params=pltpu.CompilerParams(
             collective_id=0, has_side_effects=True, vmem_limit_bytes=50 * 2**20

time: 97.3 us -> 88.3 us (0.908)
  Pallas kernels: 91.9 us -> 83 us
    pallas_call x1, Pallas kernels: 91.9 us -> 83 us  [shards(): pl.pallas_call(body, out_shape=(pltpu.VMEM((species, ROWS, LEVELS, NX), f...]
where the time goes in v4:
time: 88.3 us; the launch traced here: 88.1 us
  Pallas kernels  83 us (94%)
  local copies, waits for them, and re-layouts  4.46 us (5%)
    pallas_call x1, Pallas kernels, shards(): pl.pallas_call(body, out_shape=(pltpu.VMEM((species, ROWS, LEVELS, NX), f...  83 us
    unnamed x2, local copies, waits for them, and re-layouts  4.46 us

profile of v4, /device:TPU:1, one launch (start us, length us, event | category | flops | bytes accessed | tf_op | source)
XLA Modules:
  0.0 88.1 jit_solution(17552046972734456608)
XLA Ops:
  0.6 83.0 %shard_map.68 = (f32[32,6,8,1440]{3,2,1,0:T(8,128)S(1)}, f32[6,8,1440]{2,1,0:T(8,128)S(1)}) custom-call(f32[32,6,8,1440]{3,2,1,0:T(8,128)} %bitcast.8, f32[6,1,1440]{2,1,0:T(1,128)} %bitcast.9, f32[6,1,1440]{2,1,0:T(1,128)} %bitcast.10, f32[6,1,1440]{2,1,0:T(1,128)} %bitcast.11, s32[96]{0:T(128)} %refs_4_.1), custom_call_target="tpu_custom_call" | custom-call | flops 1000000000 | bytes 20000000 | tf_op jit(solution)/shard_map/pallas_call | solution.py:679
  83.7 3.7 %copy.9 = f32[32,8,6,1440]{3,1,2,0:T(8,128)} copy(f32[32,8,6,1440]{3,1,2,0:T(8,128)S(1)} %bitcast.6) | data formatting | bytes 17694720
  87.4 0.7 copy.10

commit v5 on v4

--- a/solution.py
+++ b/solution.py
@@ -24,6 +24,7 @@
 USED = NX // COLS
 SPARE = LANES - USED
 SLOTS = USED // SPARE
+COPIES = 4
 ROW_SETS = PIECE * 2
 DENSE = ROW_SETS * COLS * USED // LANES
 PACK = LANES // LEVELS
@@ -604,6 +605,14 @@
     def near_row(row):
         return odd * row + (1 - odd) * (1 - row)
 
+    def near_piece(piece):
+        def block(col, carry):
+            for k in range(PIECE):
+                merid_near(piece * PIECE + k, col)
+            return carry
+
+        lax.fori_loop(0, COLS, block, 0, unroll=2)
+
     def near_group(group, swept_already):
         part = pl.ds(group * GROUP, GROUP)
 
@@ -613,6 +622,7 @@
                 across(group * EACH + k, swept_already).wait()
                 if swept_already:
                     unpack_piece(group * EACH + k)
+                    near_piece(group * EACH + k)
                 return inside
 
             lax.fori_loop(0, EACH, arrive, 0)
@@ -642,7 +652,14 @@
 
             lax.fori_loop(0, GROUP, same, 0)
 
-        merid_all(group, merid_near, 4)
+        if swept_already:
+
+            @pl.when(jnp.logical_not(has_outer))
+            def _():
+                merid_all(group, merid_near, 4)
+
+        else:
+            merid_all(group, merid_near, 4)
 
         def back(row, inside):
             turn_out(lambda col: swept[part, row, col], write_out(part, row), GROUP)
@@ -660,6 +677,18 @@
 
     lax.fori_loop(0, RAW_GROUPS, near_raw, 0)
     lax.fori_loop(RAW_GROUPS, groups, near_swept, 0)
+
+
+def store(ratios, masses, out, mass_out, sems):
+    each = ratios.shape[0] // COPIES
+    copies = [pltpu.make_async_copy(masses, mass_out, sems.at[COPIES])]
+    for k in range(COPIES):
+        part = pl.ds(k * each, each)
+        copies.append(pltpu.make_async_copy(ratios.at[part], out.at[part], sems.at[k]))
+    for copy in copies:
+        copy.start()
+    for copy in copies:
+        copy.wait()
 
 
 def shards(tiles, tracer, air_mass, zonal_flux, meridional_flux, substeps):
@@ -737,6 +766,17 @@
         ),
         cost_estimate=pl.CostEstimate(flops=10**9, bytes_accessed=2 * 10**7, transcendentals=0),
     )(jnp.transpose(tracer, (0, 2, 1, 3)), *rows_first, substeps)
+    ratios, masses = pl.pallas_call(
+        store,
+        out_shape=(
+            jax.ShapeDtypeStruct((species, ROWS, LEVELS, NX), f32),
+            jax.ShapeDtypeStruct((ROWS, LEVELS, NX), f32),
+        ),
+        in_specs=[vmem, vmem],
+        out_specs=(pl.BlockSpec(memory_space=pl.ANY), pl.BlockSpec(memory_space=pl.ANY)),
+        scratch_shapes=[dma((COPIES + 1,))],
+        compiler_params=pltpu.CompilerParams(vmem_limit_bytes=16 * 2**20),
+    )(ratios, masses)
     return jnp.transpose(ratios, (0, 2, 1, 3)), jnp.transpose(masses, (1, 0, 2))
 
 

time: 88.3 us -> 86.9 us (0.984)
  local copies, waits for them, and re-layouts: 4.46 us -> 0 us
  Pallas kernels: 83 us -> 86.1 us
    unnamed x2 -> x0, local copies, waits for them, and re-layouts: 4.46 us -> none
    pallas_call x0 -> x1, Pallas kernels: none -> 3.81 us  [shards(): pl.pallas_call(store, out_shape=(jax.ShapeDtypeStruct((species, ROWS, LEV...]
where the time goes in v5:
time: 86.9 us; the launch traced here: 86.7 us
  Pallas kernels  86.1 us (99%)
    pallas_call x1, Pallas kernels, shards(): pl.pallas_call(body, out_shape=(pltpu.VMEM((species, ROWS, LEVELS, NX), f...  82.3 us
    pallas_call x1, Pallas kernels, shards(): pl.pallas_call(store, out_shape=(jax.ShapeDtypeStruct((species, ROWS, LEV...  3.81 us

profile of v5, /device:TPU:1, one launch (start us, length us, event | category | flops | bytes accessed | tf_op | source)
XLA Modules:
  0.0 86.7 jit_solution(7968720292864568398)
XLA Ops:
  0.6 82.3 %shard_map.68 = (f32[32,6,8,1440]{3,2,1,0:T(8,128)S(1)}, f32[6,8,1440]{2,1,0:T(8,128)S(1)}) custom-call(f32[32,6,8,1440]{3,2,1,0:T(8,128)} %bitcast.6, f32[6,1,1440]{2,1,0:T(1,128)} %bitcast.7, f32[6,1,1440]{2,1,0:T(1,128)} %bitcast.8, f32[6,1,1440]{2,1,0:T(1,128)} %bitcast.9, s32[96]{0:T(128)} %refs_4_.1), custom_call_target="tpu_custom_call" | custom-call | flops 1000000000 | bytes 20000000 | tf_op jit(solution)/shard_map/pallas_call | solution.py:708
  82.9 3.8 %shard_map.69 = (f32[32,6,8,1440]{3,2,1,0:T(8,128)}, f32[6,8,1440]{2,1,0:T(8,128)}) custom-call(f32[32,6,8,1440]{3,2,1,0:T(8,128)S(1)} %get-tuple-element.6.ratios, f32[6,8,1440]{2,1,0:T(8,128)S(1)} %get-tuple-element.7.masses), custom_call_target="tpu_custom_call" | custom-call | tf_op jit(solution)/shard_map/pallas_call | solution.py:769

commit v6 on v5

--- a/solution.py
+++ b/solution.py
@@ -278,14 +278,11 @@
                     axis=1,
                 )
 
+    send_across(0, False)
+    pass_on(first_kind)
+    send_across(1, False)
+    send_across(2, False)
     give_own(more_kind)
-    for piece in range(1):
-        send_across(piece, False)
-    pass_on(first_kind)
-    pass_on(more_kind)
-
-    for piece in range(1, 3):
-        send_across(piece, False)
     pl.when(has_outer)(lambda: rest_across().start())
 
     for buffer in (turned, turned_more):
@@ -325,6 +322,7 @@
         return carry
 
     lax.fori_loop(0, packs * ROWS, turn_one, 0)
+    pass_on(more_kind)
     settle(first_kind)
 
     def turn_fields(source, level_ref, rows):

time: 86.9 us -> 86.9 us (level)
  no operation moved by 1% of the time
where the time goes in v6:
time: 86.9 us; the launch traced here: 86.7 us
  Pallas kernels  86.1 us (99%)
    pallas_call x1, Pallas kernels, shards(): pl.pallas_call(body, out_shape=(pltpu.VMEM((species, ROWS, LEVELS, NX), f...  82.3 us
    pallas_call x1, Pallas kernels, shards(): pl.pallas_call(store, out_shape=(jax.ShapeDtypeStruct((species, ROWS, LEV...  3.81 us

profile of v6, /device:TPU:1, one launch (start us, length us, event | category | flops | bytes accessed | tf_op | source)
XLA Modules:
  0.0 86.7 jit_solution(3748693184115220608)
XLA Ops:
  0.6 82.3 %shard_map.68 = (f32[32,6,8,1440]{3,2,1,0:T(8,128)S(1)}, f32[6,8,1440]{2,1,0:T(8,128)S(1)}) custom-call(f32[32,6,8,1440]{3,2,1,0:T(8,128)} %bitcast.6, f32[6,1,1440]{2,1,0:T(1,128)} %bitcast.7, f32[6,1,1440]{2,1,0:T(1,128)} %bitcast.8, f32[6,1,1440]{2,1,0:T(1,128)} %bitcast.9, s32[96]{0:T(128)} %refs_4_.1), custom_call_target="tpu_custom_call" | custom-call | flops 1000000000 | bytes 20000000 | tf_op jit(solution)/shard_map/pallas_call | solution.py:706
  82.9 3.8 %shard_map.69 = (f32[32,6,8,1440]{3,2,1,0:T(8,128)}, f32[6,8,1440]{2,1,0:T(8,128)}) custom-call(f32[32,6,8,1440]{3,2,1,0:T(8,128)S(1)} %get-tuple-element.6.ratios, f32[6,8,1440]{2,1,0:T(8,128)S(1)} %get-tuple-element.7.masses), custom_call_target="tpu_custom_call" | custom-call | tf_op jit(solution)/shard_map/pallas_call | solution.py:767
